TPU v7x, 32 devices: a whole 2x2x4 slice. The times are simulated.
32 devices in a mesh: blk: 16 (over z, x, core), batch: 2 (over y).
Axes of the slice: x: 2, y: 2, z: 4, core: 2. Of those that a mesh axis runs over, the one named last changes fastest.
Arguments:
- residues: bfloat16 [2, 2048, 512], P('batch', 'blk'), may hold values from -6 to 6
- memory: bfloat16 [2, 2048, 512], P('batch', 'blk'), may hold values from -6 to 6
- lengths: int32 [2, 4], P('batch'), may hold values from 1 to 2000, as said below
- cotangent: bfloat16 [2, 2048, 512], P('batch', 'blk'), may hold values from -6 to 6
- self_norm_gain: float32 [512], replicated, may hold values from 0.5 to 1.5
- self_norm_bias: float32 [512], replicated, may hold values from -3 to 3
- self_query: bfloat16 [512, 512], replicated, may hold values from -0.25 to 0.25
- self_query_bias: float32 [512], replicated, may hold values from -3 to 3
- self_key: bfloat16 [512, 512], replicated, may hold values from -0.25 to 0.25
- self_value: bfloat16 [512, 512], replicated, may hold values from -0.25 to 0.25
- self_value_bias: float32 [512], replicated, may hold values from -0.6 to 0.6
- self_output: bfloat16 [512, 512], replicated, may hold values from -4 to 4
- self_output_bias: float32 [512], replicated, may hold values from -3 to 3
- cross_norm_gain: float32 [512], replicated, may hold values from 0.5 to 1.5
- cross_norm_bias: float32 [512], replicated, may hold values from -3 to 3
- cross_query: bfloat16 [512, 512], replicated, may hold values from -0.25 to 0.25
- cross_query_bias: float32 [512], replicated, may hold values from -3 to 3
- cross_key: bfloat16 [512, 512], replicated, may hold values from -0.25 to 0.25
- cross_value: bfloat16 [512, 512], replicated, may hold values from -0.25 to 0.25
- cross_value_bias: float32 [512], replicated, may hold values from -0.6 to 0.6
- cross_output: bfloat16 [512, 512], replicated, may hold values from -4 to 4
- cross_output_bias: float32 [512], replicated, may hold values from -3 to 3
- feed_norm_gain: float32 [512], replicated, may hold values from 0.1 to 1.9
- feed_norm_bias: float32 [512], replicated, may hold values from -3 to 3
- feed_in: bfloat16 [512, 2048], replicated, may hold values from -0.25 to 0.25
- feed_in_bias: float32 [2048], replicated, may hold values from -3 to 3
- feed_out: bfloat16 [2048, 512], replicated, may hold values from -0.125 to 0.125
- feed_out_bias: float32 [512], replicated, may hold values from -6 to 6
Outputs:
- layer_out: float32 [2, 2048, 512], P('batch', 'blk')
- residues_grad: float32 [2, 2048, 512], P('batch', 'blk')
- memory_grad: float32 [2, 2048, 512], P('batch', 'blk')
- grad_self_norm_gain: float32 [512], P('blk')
- grad_self_norm_bias: float32 [512], P('blk')
- grad_self_query: float32 [512, 512], P('blk')
- grad_self_query_bias: float32 [512], P('blk')
- grad_self_key: float32 [512, 512], P('blk')
- grad_self_value: float32 [512, 512], P('blk')
- grad_self_value_bias: float32 [512], P('blk')
- grad_self_output: float32 [512, 512], P('blk')
- grad_self_output_bias: float32 [512], P('blk')
- grad_cross_norm_gain: float32 [512], P('blk')
- grad_cross_norm_bias: float32 [512], P('blk')
- grad_cross_query: float32 [512, 512], P('blk')
- grad_cross_query_bias: float32 [512], P('blk')
- grad_cross_key: float32 [512, 512], P('blk')
- grad_cross_value: float32 [512, 512], P('blk')
- grad_cross_value_bias: float32 [512], P('blk')
- grad_cross_output: float32 [512, 512], P('blk')
- grad_cross_output_bias: float32 [512], P('blk')
- grad_feed_norm_gain: float32 [512], P('blk')
- grad_feed_norm_bias: float32 [512], P('blk')
- grad_feed_in: float32 [512, 2048], P('blk')
- grad_feed_in_bias: float32 [2048], P('blk')
- grad_feed_out: float32 [2048, 512], P('blk')
- grad_feed_out_bias: float32 [512], P('blk')
Inputs may be any that keep to these rules, and one draw needn't show every extreme that they name: Each row of lengths sums to 2048 and holds positive counts. In every group one complex, at a position that varies, has exactly 2048 - 3 * (16) residues, so it begins within the first 128 residues and ends within the last 128; the shortest complex of every group has 1 residue.
All inputs are finite; a program needn't handle non-finite values.
Results may differ from a plain program's by a relative error of at most 0.034.
Values may be sent and summed in bfloat16 or wider, within the bound.
A program may use at most 384 MiB of HBM per device.

v0:
```python
import jax
import jax.numpy as jnp
from jax import lax
from jax.sharding import PartitionSpec as P

HEADS = 8


NEG = -1e30
EPS = 1e-05
SQRT_HALF = 0.7071067811865476
INV_ROOT_TAU = 0.3989422804014327


def layer_norm(values, gain, shift):
    average = jnp.mean(values, -1, keepdims=True)
    centred = values - average
    factor = lax.rsqrt(jnp.mean(centred * centred, -1, keepdims=True) + EPS)
    normal = centred * factor
    return (normal * gain + shift, normal, factor)


def norm_back(gradient, normal, factor, gain):
    weighted = gradient * gain
    average_one = jnp.mean(weighted, -1, keepdims=True)
    average_two = jnp.mean(weighted * normal, -1, keepdims=True)
    return (
        factor * (weighted - average_one - normal * average_two),
        jnp.sum(gradient * normal, 0),
        jnp.sum(gradient, 0),
    )


def gelu_value(values):
    return 0.5 * values * (1.0 + lax.erf(values * SQRT_HALF))


def gelu_slope(values):
    return (
        0.5 * (1.0 + lax.erf(values * SQRT_HALF))
        + values * jnp.exp(-0.5 * values * values) * INV_ROOT_TAU
    )


def heads_of(matrix):
    return matrix.reshape(matrix.shape[0], HEADS, -1)


def complex_ids(lengths_row, positions):
    bounds = jnp.cumsum(lengths_row)
    return jnp.sum((positions[:, None] >= bounds[None, :]).astype(jnp.int32), 1)


def visible(query_pos, query_doc, key_pos, key_doc, causal):
    allowed = query_doc[:, None] == key_doc[None, :]
    if causal:
        allowed = allowed & (key_pos[None, :] <= query_pos[:, None])
    return allowed


def project(left, right):
    return jnp.dot(left, right, preferred_element_type=jnp.float32)


def pass_through(pieces):
    return (pieces[0].astype(jnp.bfloat16), pieces[1].astype(jnp.bfloat16))


def empty_state(tokens, head_size):
    return (
        jnp.full((HEADS, tokens), NEG, jnp.float32),
        jnp.zeros((HEADS, tokens), jnp.float32),
        jnp.zeros((HEADS, tokens, head_size), jnp.float32),
    )


def finish(state_out):
    running_max, running_sum, summed = state_out
    attended = (summed / running_sum[..., None]).transpose(1, 0, 2)
    return (attended.reshape(attended.shape[0], -1), (running_max + jnp.log(running_sum)).T)


def spread_of(grad_low, attended):
    return jnp.sum(heads_of(grad_low).astype(jnp.float32) * heads_of(attended), -1)


def forward_fold(queries, query_pos, query_doc, lengths_row, causal, prepare, carried, pieces):
    factor = queries.shape[-1] ** (-0.5)
    piece_rows = pieces[0].shape[0]
    key_pos = jnp.arange(piece_rows, dtype=jnp.int32)
    allowed = visible(query_pos, query_doc, key_pos, complex_ids(lengths_row, key_pos), causal)

    def active(state_in):
        running_max, running_sum, summed = state_in
        key_rows, value_rows = prepare(pieces)
        scores = (
            jnp.einsum(
                "qhd,khd->hqk", queries, heads_of(key_rows), preferred_element_type=jnp.float32
            )
            * factor
        )
        scores = jnp.where(allowed[None], scores, NEG)
        new_max = jnp.maximum(running_max, jnp.max(scores, -1))
        weights = jnp.where(allowed[None], jnp.exp(scores - new_max[..., None]), 0.0)
        running_sum = jnp.sum(weights, -1)
        summed = jnp.einsum(
            "hqk,khd->hqd",
            weights.astype(jnp.bfloat16),
            heads_of(value_rows),
            preferred_element_type=jnp.float32,
        )
        return (new_max, running_sum, summed)

    return lax.cond(jnp.any(allowed), active, lambda state_in: state_in, carried)


def query_fold(
    queries, grad_out, log_total, spread, query_pos, query_doc, lengths_row, causal, prepare
):
    factor = queries.shape[-1] ** (-0.5)
    log_rows = log_total.T[..., None]
    spread_rows = spread.T[..., None]

    def fold(carried, pieces, offset):
        piece_rows = pieces[0].shape[0]
        key_pos = jnp.arange(piece_rows, dtype=jnp.int32)
        allowed = visible(query_pos, query_doc, key_pos, complex_ids(lengths_row, key_pos), causal)

        def active(accum):
            key_rows, value_rows = prepare(pieces)
            key_heads = heads_of(key_rows)
            scores = (
                jnp.einsum("qhd,khd->hqk", queries, key_heads, preferred_element_type=jnp.float32)
                * factor
            )
            scores = jnp.where(allowed[None], scores, NEG)
            weights = jnp.where(allowed[None], jnp.exp(scores - log_rows), 0.0)
            slopes = jnp.einsum(
                "qhd,khd->hqk", grad_out, heads_of(value_rows), preferred_element_type=jnp.float32
            )
            tilted = (weights * (slopes - spread_rows)).astype(jnp.bfloat16)
            return (
                jnp.einsum("hqk,khd->qhd", tilted, key_heads, preferred_element_type=jnp.float32)
                * factor
            )

        return lax.cond(jnp.any(allowed), active, lambda accum: accum, carried)

    return fold


def key_fold(key_heads, value_heads, key_pos, key_doc, lengths_row, causal):
    factor = key_heads.shape[-1] ** (-0.5)

    def fold(carried, pieces, offset):
        queries, grad_out, log_total, spread = pieces
        piece_rows = queries.shape[0]
        query_pos = jnp.arange(piece_rows, dtype=jnp.int32)
        allowed = visible(query_pos, complex_ids(lengths_row, query_pos), key_pos, key_doc, causal)

        def active(sums_in):
            query_heads = heads_of(queries.astype(jnp.bfloat16))
            grad_heads = heads_of(grad_out.astype(jnp.bfloat16))
            scores = (
                jnp.einsum(
                    "qhd,khd->hqk", query_heads, key_heads, preferred_element_type=jnp.float32
                )
                * factor
            )
            scores = jnp.where(allowed[None], scores, NEG)
            weights = jnp.where(allowed[None], jnp.exp(scores - log_total.T[..., None]), 0.0)
            grad_values = jnp.einsum(
                "hqk,qhd->khd",
                weights.astype(jnp.bfloat16),
                grad_heads,
                preferred_element_type=jnp.float32,
            )
            slopes = jnp.einsum(
                "qhd,khd->hqk", grad_heads, value_heads, preferred_element_type=jnp.float32
            )
            tilted = (weights * (slopes - spread.T[..., None])).astype(jnp.bfloat16)
            grad_keys = (
                jnp.einsum("hqk,qhd->khd", tilted, query_heads, preferred_element_type=jnp.float32)
                * factor
            )
            return (grad_keys, grad_values)

        return lax.cond(jnp.any(allowed), active, lambda sums_in: sums_in, carried)

    return fold


def mutual_fold(
    queries,
    grad_out,
    log_total,
    spread,
    key_heads,
    value_heads,
    positions,
    docs,
    lengths_row,
    carried,
    pieces,
    offset,
):
    toward_queries = query_fold(
        queries, grad_out, log_total, spread, positions, docs, lengths_row, True, pass_through
    )
    toward_keys = key_fold(key_heads, value_heads, positions, docs, lengths_row, True)
    grad_query_acc, grad_keys, grad_values = carried
    remote_q, remote_grad, remote_log, remote_spread, remote_k, remote_v = pieces
    grad_query_acc = toward_queries(grad_query_acc, (remote_k, remote_v), offset)
    grad_keys, grad_values = toward_keys(
        (grad_keys, grad_values), (remote_q, remote_grad, remote_log, remote_spread), offset
    )
    return (grad_query_acc, grad_keys, grad_values)


def local(
    residues,
    memory,
    lengths,
    cotangent,
    self_norm_gain,
    self_norm_bias,
    self_query,
    self_query_bias,
    self_key,
    self_value,
    self_value_bias,
    self_output,
    self_output_bias,
    cross_norm_gain,
    cross_norm_bias,
    cross_query,
    cross_query_bias,
    cross_key,
    cross_value,
    cross_value_bias,
    cross_output,
    cross_output_bias,
    feed_norm_gain,
    feed_norm_bias,
    feed_in,
    feed_in_bias,
    feed_out,
    feed_out_bias,
):
    tokens = residues.shape[1]
    model_width = residues.shape[2]
    head_size = model_width // HEADS
    device_rank = lax.axis_index("blk")
    positions = device_rank * tokens + jnp.arange(tokens, dtype=jnp.int32)
    lengths_row = lengths[0]
    complexes = complex_ids(lengths_row, positions)
    inputs = residues[0].astype(jnp.float32)
    encoded = memory[0]
    upstream = cotangent[0].astype(jnp.float32)
    normed_one, unit_one, factor_one = layer_norm(inputs, self_norm_gain, self_norm_bias)
    normed_one = normed_one.astype(jnp.bfloat16)
    self_q = (project(normed_one, self_query) + self_query_bias).astype(jnp.bfloat16)
    self_k = project(normed_one, self_key).astype(jnp.bfloat16)
    self_v = (project(normed_one, self_value) + self_value_bias).astype(jnp.bfloat16)
    state_out = forward_fold(
        heads_of(self_q),
        positions,
        complexes,
        lengths_row,
        True,
        pass_through,
        empty_state(tokens, head_size),
        (
            lax.all_gather(self_k, "blk", axis=0, tiled=True),
            lax.all_gather(self_v, "blk", axis=0, tiled=True),
        ),
    )
    self_attended, self_log = finish(state_out)
    self_low = self_attended.astype(jnp.bfloat16)
    after_self = inputs + project(self_low, self_output) + self_output_bias
    normed_two, unit_two, factor_two = layer_norm(after_self, cross_norm_gain, cross_norm_bias)
    normed_two = normed_two.astype(jnp.bfloat16)
    cross_q = (project(normed_two, cross_query) + cross_query_bias).astype(jnp.bfloat16)
    cross_k = project(encoded, cross_key).astype(jnp.bfloat16)
    cross_v = (project(encoded, cross_value) + cross_value_bias).astype(jnp.bfloat16)
    state_out = forward_fold(
        heads_of(cross_q),
        positions,
        complexes,
        lengths_row,
        False,
        pass_through,
        empty_state(tokens, head_size),
        (
            lax.all_gather(cross_k, "blk", axis=0, tiled=True),
            lax.all_gather(cross_v, "blk", axis=0, tiled=True),
        ),
    )
    cross_attended, cross_log = finish(state_out)
    cross_low = cross_attended.astype(jnp.bfloat16)
    after_cross = after_self + project(cross_low, cross_output) + cross_output_bias
    normed_three, unit_three, factor_three = layer_norm(after_cross, feed_norm_gain, feed_norm_bias)
    normed_three = normed_three.astype(jnp.bfloat16)
    inner = project(normed_three, feed_in) + feed_in_bias
    activation = gelu_value(inner).astype(jnp.bfloat16)
    layer_out = after_cross + project(activation, feed_out) + feed_out_bias
    grad_branch = upstream.astype(jnp.bfloat16)
    grad_feed_out_bias = jnp.sum(grad_branch.astype(jnp.float32), 0)
    grad_feed_out = jnp.einsum(
        "tf,td->fd", activation, grad_branch, preferred_element_type=jnp.float32
    )
    grad_active = jnp.einsum("td,fd->tf", grad_branch, feed_out, preferred_element_type=jnp.float32)
    grad_inner = (grad_active * gelu_slope(inner)).astype(jnp.bfloat16)
    grad_feed_in_bias = jnp.sum(grad_inner.astype(jnp.float32), 0)
    grad_feed_in = jnp.einsum(
        "td,tf->df", normed_three, grad_inner, preferred_element_type=jnp.float32
    )
    grad_normed = jnp.einsum("tf,df->td", grad_inner, feed_in, preferred_element_type=jnp.float32)
    norm_grad, grad_feed_norm_gain, grad_feed_norm_bias = norm_back(
        grad_normed, unit_three, factor_three, feed_norm_gain
    )
    upstream_two = upstream + norm_grad
    feed_parts = (
        grad_feed_norm_gain,
        grad_feed_norm_bias,
        grad_feed_in,
        grad_feed_in_bias,
        grad_feed_out,
        grad_feed_out_bias,
    )
    grad_branch = upstream_two.astype(jnp.bfloat16)
    grad_cross_output_bias = jnp.sum(grad_branch.astype(jnp.float32), 0)
    grad_cross_output = jnp.einsum(
        "tc,te->ce", cross_low, grad_branch, preferred_element_type=jnp.float32
    )
    grad_attended = jnp.einsum(
        "te,ce->tc", grad_branch, cross_output, preferred_element_type=jnp.float32
    ).astype(jnp.bfloat16)
    spread = spread_of(grad_attended, cross_attended)
    query_start = jnp.zeros((tokens, HEADS, head_size), jnp.float32)
    grad_query_acc = query_fold(
        heads_of(cross_q),
        heads_of(grad_attended),
        cross_log,
        spread,
        positions,
        complexes,
        lengths_row,
        False,
        pass_through,
    )(
        query_start,
        (
            lax.all_gather(cross_k, "blk", axis=0, tiled=True),
            lax.all_gather(cross_v, "blk", axis=0, tiled=True),
        ),
        jnp.int32(0),
    )
    grad_keys_acc, grad_values_acc = key_fold(
        heads_of(cross_k), heads_of(cross_v), positions, complexes, lengths_row, False
    )(
        (query_start, query_start),
        (
            lax.all_gather(cross_q.astype(jnp.float32), "blk", axis=0, tiled=True),
            lax.all_gather(grad_attended.astype(jnp.float32), "blk", axis=0, tiled=True),
            lax.all_gather(cross_log, "blk", axis=0, tiled=True),
            lax.all_gather(spread, "blk", axis=0, tiled=True),
        ),
        jnp.int32(0),
    )
    grad_cq = grad_query_acc.reshape(tokens, model_width).astype(jnp.bfloat16)
    grad_ck = grad_keys_acc.reshape(tokens, model_width).astype(jnp.bfloat16)
    grad_cv = grad_values_acc.reshape(tokens, model_width).astype(jnp.bfloat16)
    grad_cross_query = jnp.einsum(
        "tc,te->ce", normed_two, grad_cq, preferred_element_type=jnp.float32
    )
    grad_cross_query_bias = jnp.sum(grad_cq.astype(jnp.float32), 0)
    grad_cross_key = jnp.einsum("tc,te->ce", encoded, grad_ck, preferred_element_type=jnp.float32)
    grad_cross_value = jnp.einsum("tc,te->ce", encoded, grad_cv, preferred_element_type=jnp.float32)
    grad_cross_value_bias = jnp.sum(grad_cv.astype(jnp.float32), 0)
    memory_grad = jnp.einsum(
        "te,ce->tc", grad_ck, cross_key, preferred_element_type=jnp.float32
    ) + jnp.einsum("te,ce->tc", grad_cv, cross_value, preferred_element_type=jnp.float32)
    grad_normed = jnp.einsum("te,ce->tc", grad_cq, cross_query, preferred_element_type=jnp.float32)
    norm_grad, grad_cross_norm_gain, grad_cross_norm_bias = norm_back(
        grad_normed, unit_two, factor_two, cross_norm_gain
    )
    upstream_one = upstream_two + norm_grad
    cross_parts = (
        grad_cross_norm_gain,
        grad_cross_norm_bias,
        grad_cross_query,
        grad_cross_query_bias,
        grad_cross_key,
        grad_cross_value,
        grad_cross_value_bias,
        grad_cross_output,
        grad_cross_output_bias,
    )
    grad_branch = upstream_one.astype(jnp.bfloat16)
    grad_self_output_bias = jnp.sum(grad_branch.astype(jnp.float32), 0)
    grad_self_output = jnp.einsum(
        "tc,te->ce", self_low, grad_branch, preferred_element_type=jnp.float32
    )
    grad_attended = jnp.einsum(
        "te,ce->tc", grad_branch, self_output, preferred_element_type=jnp.float32
    ).astype(jnp.bfloat16)
    spread = spread_of(grad_attended, self_attended)
    grad_query_acc, grad_keys_acc, grad_values_acc = mutual_fold(
        heads_of(self_q),
        heads_of(grad_attended),
        self_log,
        spread,
        heads_of(self_k),
        heads_of(self_v),
        positions,
        complexes,
        lengths_row,
        (query_start, query_start, query_start),
        (
            lax.all_gather(self_q.astype(jnp.float32), "blk", axis=0, tiled=True),
            lax.all_gather(grad_attended.astype(jnp.float32), "blk", axis=0, tiled=True),
            lax.all_gather(self_log, "blk", axis=0, tiled=True),
            lax.all_gather(spread, "blk", axis=0, tiled=True),
            lax.all_gather(self_k.astype(jnp.float32), "blk", axis=0, tiled=True),
            lax.all_gather(self_v.astype(jnp.float32), "blk", axis=0, tiled=True),
        ),
        jnp.int32(0),
    )
    grad_sq = grad_query_acc.reshape(tokens, model_width).astype(jnp.bfloat16)
    grad_sk = grad_keys_acc.reshape(tokens, model_width).astype(jnp.bfloat16)
    grad_sv = grad_values_acc.reshape(tokens, model_width).astype(jnp.bfloat16)
    grad_self_query = jnp.einsum(
        "tc,te->ce", normed_one, grad_sq, preferred_element_type=jnp.float32
    )
    grad_self_query_bias = jnp.sum(grad_sq.astype(jnp.float32), 0)
    grad_self_key = jnp.einsum("tc,te->ce", normed_one, grad_sk, preferred_element_type=jnp.float32)
    grad_self_value = jnp.einsum(
        "tc,te->ce", normed_one, grad_sv, preferred_element_type=jnp.float32
    )
    grad_self_value_bias = jnp.sum(grad_sv.astype(jnp.float32), 0)
    grad_normed = (
        jnp.einsum("te,ce->tc", grad_sq, self_query, preferred_element_type=jnp.float32)
        + jnp.einsum("te,ce->tc", grad_sk, self_key, preferred_element_type=jnp.float32)
        + jnp.einsum("te,ce->tc", grad_sv, self_value, preferred_element_type=jnp.float32)
    )
    norm_grad, grad_self_norm_gain, grad_self_norm_bias = norm_back(
        grad_normed, unit_one, factor_one, self_norm_gain
    )
    residues_grad = upstream_one + norm_grad
    self_parts = (
        grad_self_norm_gain,
        grad_self_norm_bias,
        grad_self_query,
        grad_self_query_bias,
        grad_self_key,
        grad_self_value,
        grad_self_value_bias,
        grad_self_output,
        grad_self_output_bias,
    )
    ordered = (
        lax.psum_scatter(self_parts[0], "blk", scatter_dimension=0, tiled=True),
        lax.psum_scatter(self_parts[1], "blk", scatter_dimension=0, tiled=True),
        lax.psum_scatter(self_parts[2], "blk", scatter_dimension=0, tiled=True),
        lax.psum_scatter(self_parts[3], "blk", scatter_dimension=0, tiled=True),
        lax.psum_scatter(self_parts[4], "blk", scatter_dimension=0, tiled=True),
        lax.psum_scatter(self_parts[5], "blk", scatter_dimension=0, tiled=True),
        lax.psum_scatter(self_parts[6], "blk", scatter_dimension=0, tiled=True),
        lax.psum_scatter(self_parts[7], "blk", scatter_dimension=0, tiled=True),
        lax.psum_scatter(self_parts[8], "blk", scatter_dimension=0, tiled=True),
        lax.psum_scatter(cross_parts[0], "blk", scatter_dimension=0, tiled=True),
        lax.psum_scatter(cross_parts[1], "blk", scatter_dimension=0, tiled=True),
        lax.psum_scatter(cross_parts[2], "blk", scatter_dimension=0, tiled=True),
        lax.psum_scatter(cross_parts[3], "blk", scatter_dimension=0, tiled=True),
        lax.psum_scatter(cross_parts[4], "blk", scatter_dimension=0, tiled=True),
        lax.psum_scatter(cross_parts[5], "blk", scatter_dimension=0, tiled=True),
        lax.psum_scatter(cross_parts[6], "blk", scatter_dimension=0, tiled=True),
        lax.psum_scatter(cross_parts[7], "blk", scatter_dimension=0, tiled=True),
        lax.psum_scatter(cross_parts[8], "blk", scatter_dimension=0, tiled=True),
        lax.psum_scatter(feed_parts[0], "blk", scatter_dimension=0, tiled=True),
        lax.psum_scatter(feed_parts[1], "blk", scatter_dimension=0, tiled=True),
        lax.psum_scatter(feed_parts[2], "blk", scatter_dimension=0, tiled=True),
        lax.psum_scatter(feed_parts[3], "blk", scatter_dimension=0, tiled=True),
        lax.psum_scatter(feed_parts[4], "blk", scatter_dimension=0, tiled=True),
        lax.psum_scatter(feed_parts[5], "blk", scatter_dimension=0, tiled=True),
    )
    totals = lax.psum(
        (
            ordered[0],
            ordered[1],
            ordered[2],
            ordered[3],
            ordered[4],
            ordered[5],
            ordered[6],
            ordered[7],
            ordered[8],
            ordered[9],
            ordered[10],
            ordered[11],
            ordered[12],
            ordered[13],
            ordered[14],
            ordered[15],
            ordered[16],
            ordered[17],
            ordered[18],
            ordered[19],
            ordered[20],
            ordered[21],
            ordered[22],
            ordered[23],
        ),
        "batch",
    )
    return (layer_out[None], residues_grad[None], memory_grad[None]) + tuple(totals)


def solution(mesh):
    return jax.shard_map(
        local,
        mesh=mesh,
        in_specs=(
            P("batch", "blk", None),
            P("batch", "blk", None),
            P("batch", None),
            P("batch", "blk", None),
            P(),
            P(),
            P(),
            P(),
            P(),
            P(),
            P(),
            P(),
            P(),
            P(),
            P(),
            P(),
            P(),
            P(),
            P(),
            P(),
            P(),
            P(),
            P(),
            P(),
            P(),
            P(),
            P(),
            P(),
        ),
        out_specs=(
            P("batch", "blk", None),
            P("batch", "blk", None),
            P("batch", "blk", None),
            P("blk"),
            P("blk"),
            P("blk", None),
            P("blk"),
            P("blk", None),
            P("blk", None),
            P("blk"),
            P("blk", None),
            P("blk"),
            P("blk"),
            P("blk"),
            P("blk", None),
            P("blk"),
            P("blk", None),
            P("blk", None),
            P("blk"),
            P("blk", None),
            P("blk"),
            P("blk"),
            P("blk"),
            P("blk", None),
            P("blk"),
            P("blk", None),
            P("blk"),
        ),
        check_vma=False,
    )
```

profile of v0, /device:TPU:0, one launch (start us, length us, event | category | flops | bytes accessed | tf_op | source)
XLA Modules:
  0.0 1180.9 jit_solution(15279109858352485474)
XLA Ops:
  23.5 32.4 %all-gather.11.cloned.1.call-done = bf16[2048,512]{1,0:T(8,128)(2,1)} async-done(((bf16[128,512]{1,0:T(8,128)(2,1)}), bf16[2048,512]{1,0:T(8,128)(2,1)}) %all-gather.11.cloned.1.call-update) | async-done | bytes 2097168 | tf_op jit(solution)/shard_map/all_gather | solution.py:274
  55.9 42.4 %all-gather.13.cloned.1.call-done = bf16[2048,512]{1,0:T(8,128)(2,1)} async-done(((bf16[128,512]{1,0:T(8,128)(2,1)}), bf16[2048,512]{1,0:T(8,128)(2,1)}) %all-gather.13.cloned.1.call-update) | async-done | bytes 2097168 | tf_op jit(solution)/shard_map/all_gather | solution.py:275
  98.3 25.2 %conditional.6 = (f32[8,128]{1,0:T(8,128)}, f32[8,128]{1,0:T(8,128)}, f32[8,128,64]{1,2,0:T(8,128)S(1)}, f32[8,128]{1,0:T(8,128)S(1)}) conditional(s32[]{:T(128)} %convert_element_type.243, () %tuple.56, (pred[128,2048]{1,0:T(8,128)(4,1)S(1)}, bf16[2048,512]{1,0:T(8,128)(2,1)}, bf16[128,8,64]{0,2,1:T(8,128)(2,1)}, bf16[2048,512]{1,0:T(8,128)(2,1)}) %tuple.57), branch_computations={%region_6.7_spmd, %region_7.10_spmd} | conditional | flops 564132864 | bytes 72515648 | solution.py:114
  98.3 4.0 copy.124
  102.3 3.3 fusion
  106.3 2.6 copy-done.1
  108.9 3.8 fusion.2
  113.3 3.9 copy.125
  117.3 6.2 fusion.3
  128.1 12.5 %all-gather.15.cloned.1.call-done = bf16[2048,512]{1,0:T(8,128)(2,1)} async-done(((bf16[128,512]{1,0:T(8,128)(2,1)}), bf16[2048,512]{1,0:T(8,128)(2,1)}) %all-gather.15.cloned.1.call-update) | async-done | bytes 2097168 | tf_op jit(solution)/shard_map/all_gather | solution.py:295
  140.6 42.2 %all-gather.17.cloned.1.call-done = bf16[2048,512]{1,0:T(8,128)(2,1)} async-done(((bf16[128,512]{1,0:T(8,128)(2,1)}), bf16[2048,512]{1,0:T(8,128)(2,1)}) %all-gather.17.cloned.1.call-update) | async-done | bytes 2097168 | tf_op jit(solution)/shard_map/all_gather | solution.py:296
  182.8 26.0 %conditional.7 = (f32[8,128]{1,0:T(8,128)}, f32[8,128]{1,0:T(8,128)}, f32[8,128,64]{1,2,0:T(8,128)S(1)}, f32[8,128]{1,0:T(8,128)}) conditional(s32[]{:T(128)} %convert_element_type.250, () %tuple.58, (pred[128,2048]{1,0:T(8,128)(4,1)S(1)}, bf16[2048,512]{1,0:T(8,128)(2,1)}, bf16[128,8,64]{0,2,1:T(8,128)(2,1)}, bf16[2048,512]{1,0:T(8,128)(2,1)}) %tuple.188), branch_computations={%region_13.14_spmd, %region_14.17_spmd} | conditional | flops 564132864 | bytes 72515648 | solution.py:114
  183.0 4.0 copy.127
  187.0 3.3 fusion.9
  191.0 2.6 copy-done.2
  193.6 3.8 fusion.11
  198.6 4.0 copy.128
  202.6 6.2 fusion.12
  214.5 2.4 convert_reduce_fusion
  227.6 24.2 %conditional.8 = (bf16[128,8,64]{0,2,1:T(8,128)(2,1)}) conditional(s32[]{:T(128)} %convert_element_type.250, () %tuple.60, (pred[128,2048]{1,0:T(8,128)(4,1)S(1)}, bf16[2048,512]{1,0:T(8,128)(2,1)}, bf16[128,8,64]{0,2,1:T(8,128)(2,1)}, f32[8,128]{1,0:T(8,128)}, bf16[2048,512]{1,0:T(8,128)(2,1)}, /*index=5*/bf16[128,8,64]{0,2,1:T(8,128)(2,1)}, ...), branch_computations={%region_22.23_spmd, %region_23.24_spmd} | conditional | flops 820117504 | bytes 32120840 | solution.py:147
  227.8 4.0 copy.130
  231.8 6.2 fusion.129
  238.0 4.0 copy.131
  241.9 9.9 fusion.20
  257.5 2.6 compare_reduce_fusion
  260.7 20.7 %all_gather.57 = f32[2048,8]{0,1:T(8,128)} all-gather(f32[128,8]{0,1:T(8,128)} %fusion.98), channel_id=1, replica_groups=mesh['blk'=16,'batch'=2] {'blk'}, dimensions={0}, use_global_device_ids=true | all-gather | bytes 69632 | tf_op jit(solution)/shard_map/all_gather | solution.py:367
  281.5 19.4 %all_gather.55 = f32[2048,8]{0,1:T(8,128)} all-gather(f32[128,8]{0,1:T(8,128)} %bitcast.244), channel_id=1, replica_groups=mesh['blk'=16,'batch'=2] {'blk'}, dimensions={0}, use_global_device_ids=true | all-gather | bytes 69632 | tf_op jit(solution)/shard_map/all_gather | solution.py:366
  302.7 37.0 %conditional.11 = (bf16[128,512]{0,1:T(8,128)(2,1)}, bf16[128,8,64]{0,2,1:T(8,128)(2,1)}, bf16[128,512]{0,1:T(8,128)(2,1)}) conditional(s32[]{:T(128)} %convert_element_type.280, () %tuple.66, (pred[2048,128]{1,0:T(8,128)(4,1)}, bf16[2048,512]{1,0:T(8,128)(2,1)}, bf16[128,512]{1,0:T(8,128)(2,1)}, f32[2048,8]{0,1:T(8,128)}, ...), branch_computations={%region_35.36_spmd, %region_36.37_spmd} | conditional | flops 1099104256 | bytes 43974680 | solution.py:188
  303.0 4.0 copy.139
  308.6 6.2 fusion.132
  314.8 3.9 copy.141
  320.5 11.2 fusion.55
  331.7 6.4 fusion.52
  341.9 2.5 copy.145
  346.8 2.6 copy.147
  360.3 28.0 %all-gather.21.cloned.1.call-done = bf16[2048,512]{1,0:T(8,128)(2,1)} async-done(((bf16[128,512]{1,0:T(8,128)(2,1)}), bf16[2048,512]{1,0:T(8,128)(2,1)}) %all-gather.21.cloned.1.call-update) | async-done | bytes 2097168 | tf_op jit(solution)/shard_map/all_gather | solution.py:426
  388.3 35.4 %conditional.9 = (bf16[128,8,64]{0,2,1:T(8,128)(2,1)S(1)}) conditional(s32[]{:T(128)} %convert_element_type.243, () %tuple.62, (pred[128,2048]{1,0:T(8,128)(4,1)S(1)}, bf16[2048,512]{1,0:T(8,128)(2,1)}, bf16[128,8,64]{0,2,1:T(8,128)(2,1)}, f32[8,128]{1,0:T(8,128)}, bf16[2048,512]{1,0:T(8,128)(2,1)}, /*index=5*/bf16[128,8,64]{0,2,1:T(8,128)(2,1)S(1)}, ...), branch_computations={%region_27.28_spmd, %region_28.29_spmd} | conditional | flops 820117504 | bytes 32120840 | solution.py:147
  400.7 4.0 copy.133
  404.7 6.2 fusion.130
  410.9 3.9 copy.134
  414.8 9.0 fusion.26
  426.6 19.8 %all_gather.53 = f32[2048,8]{0,1:T(8,128)S(1)} all-gather(f32[128,8]{0,1:T(8,128)} %fusion.99), channel_id=1, replica_groups=mesh['blk'=16,'batch'=2] {'blk'}, dimensions={0}, use_global_device_ids=true | all-gather | bytes 69632 | tf_op jit(solution)/shard_map/all_gather | solution.py:424
  446.4 18.1 %all_gather.51 = f32[2048,8]{0,1:T(8,128)S(1)} all-gather(f32[128,8]{0,1:T(8,128)} %bitcast.245), channel_id=1, replica_groups=mesh['blk'=16,'batch'=2] {'blk'}, dimensions={0}, use_global_device_ids=true | all-gather | bytes 69632 | tf_op jit(solution)/shard_map/all_gather | solution.py:423
  464.5 8.3 all-gather.25.cloned.1.call-done
  472.9 33.7 %conditional.10 = (bf16[128,512]{0,1:T(8,128)(2,1)}, bf16[128,8,64]{0,2,1:T(8,128)(2,1)}, bf16[128,512]{0,1:T(8,128)(2,1)}) conditional(s32[]{:T(128)} %convert_element_type.273, () %tuple.64, (pred[2048,128]{1,0:T(8,128)(4,1)S(1)}, bf16[2048,512]{1,0:T(8,128)(2,1)}, bf16[128,512]{1,0:T(8,128)(2,1)S(1)}, f32[2048,8]{0,1:T(8,128)S(1)}, ...), branch_computations={%region_30.31_spmd, %region_31.32_spmd} | conditional | flops 1099104256 | bytes 43974680 | solution.py:188
  472.9 3.9 copy.135
  476.9 6.2 fusion.131
  483.2 4.0 copy.137
  487.3 11.4 fusion.39
  498.7 6.2 fusion.36
  506.5 2.5 fusion.118
  511.5 3.8 fusion.115
  515.4 3.6 fusion.101
  533.9 60.5 %all-reduce.14 = (f32[512]{0:T(512)S(1)}, f32[512]{0:T(512)S(1)}, f32[512]{0:T(512)S(1)}, f32[512]{0:T(512)S(1)}, f32[512]{0:T(512)S(1)}, /*index=5*/f32[512]{0:...) all-reduce(f32[512]{0:T(512)S(1)} %get-tuple-element.437, ...), channel_id=2, replica_groups=mesh['blk'=16,'batch'=2] {'blk'}, use_global_device_ids=true, to_apply=%region_38.39.clone | all-reduce | flops 8704 | bytes 69632
  595.5 5.5 all-reduce.15
  604.4 49.1 %reduce-scatter.23.cloned.1.call-done = f32[32,512]{1,0:T(8,128)} async-done(((f32[512,512]{1,0:T(8,128)}), f32[32,512]{1,0:T(8,128)}) %reduce-scatter.23.cloned.1.call-update) | async-done | bytes 65552 | tf_op jit(solution)/shard_map/reduce_scatter | solution.py:474
  653.4 60.4 %reduce-scatter.25.cloned.1.call-done = f32[32,512]{1,0:T(8,128)} async-done(((f32[512,512]{1,0:T(8,128)}), f32[32,512]{1,0:T(8,128)}) %reduce-scatter.25.cloned.1.call-update) | async-done | bytes 65552 | tf_op jit(solution)/shard_map/reduce_scatter | solution.py:479
  713.8 59.9 %reduce-scatter.21.cloned.1.call-done = f32[32,512]{1,0:T(8,128)} async-done(((f32[512,512]{1,0:T(8,128)}), f32[32,512]{1,0:T(8,128)}) %reduce-scatter.21.cloned.1.call-update) | async-done | bytes 65552 | tf_op jit(solution)/shard_map/reduce_scatter | solution.py:470
  773.7 60.4 %reduce-scatter.15.cloned.1.call-done = f32[32,512]{1,0:T(8,128)} async-done(((f32[512,512]{1,0:T(8,128)}), f32[32,512]{1,0:T(8,128)}) %reduce-scatter.15.cloned.1.call-update) | async-done | bytes 65552 | tf_op jit(solution)/shard_map/reduce_scatter | solution.py:465
  834.1 60.0 %reduce-scatter.17.cloned.1.call-done = f32[32,512]{1,0:T(8,128)} async-done(((f32[512,512]{1,0:T(8,128)}), f32[32,512]{1,0:T(8,128)}) %reduce-scatter.17.cloned.1.call-update) | async-done | bytes 65552 | tf_op jit(solution)/shard_map/reduce_scatter | solution.py:467
  894.1 60.3 %reduce-scatter.19.cloned.1.call-done = f32[32,512]{1,0:T(8,128)} async-done(((f32[512,512]{1,0:T(8,128)}), f32[32,512]{1,0:T(8,128)}) %reduce-scatter.19.cloned.1.call-update) | async-done | bytes 65552 | tf_op jit(solution)/shard_map/reduce_scatter | solution.py:468
  954.4 75.3 %reduce-scatter.27.cloned.1.call-done = f32[32,2048]{1,0:T(8,128)} async-done(((f32[512,2048]{1,0:T(8,128)}), f32[32,2048]{1,0:T(8,128)}) %reduce-scatter.27.cloned.1.call-update) | async-done | bytes 262160 | tf_op jit(solution)/shard_map/reduce_scatter | solution.py:483
  1029.7 75.7 %reduce-scatter.29.cloned.1.call-done = f32[128,512]{1,0:T(8,128)} async-done(((f32[2048,512]{1,0:T(8,128)}), f32[128,512]{1,0:T(8,128)}) %reduce-scatter.29.cloned.1.call-update) | async-done | bytes 262160 | tf_op jit(solution)/shard_map/reduce_scatter | solution.py:485
  1110.8 47.5 %all-reduce.19.cloned.1.call-done = (f32[32,512]{1,0:T(8,128)}, f32[32,512]{1,0:T(8,128)}, f32[32,512]{1,0:T(8,128)}, f32[32,512]{1,0:T(8,128)}, f32[32,512]{1,0...) async-done(((f32[32,512]{1,0:T(8,128)}, f32[32,512]{1,0:T(8,128)}, f32[32,512]{1,0:T(8,128)}, ...) | async-done | bytes 1048592 | tf_op jit(solution)/shard_map/psum | solution.py:488
  (234 shorter events, 111.9 us)
Async XLA Ops:
  7.2 207.3 %copy-start = (bf16[2048,512]{1,0:T(8,128)(2,1)S(1)}, bf16[2048,512]{1,0:T(8,128)(2,1)}, u32[]{:S(2)}) copy-start(bf16[2048,512]{1,0:T(8,128)(2,1)} %param.66) | copy-start | bytes 6291460
  7.2 48.6 %all-gather.11.cloned.1.call-start = ((), (), s32[]{:S(2)}) async-start(), calls=%async_computation.10 | async-start | bytes 2228224 | tf_op jit(solution)/shard_map/all_gather | solution.py:274
  8.4 89.8 %copy-start.24 = (f32[128]{0:T(128)}, f32[128]{0:T(128)S(1)}, u32[]{:S(2)}) copy-start(f32[128]{0:T(128)S(1)} %broadcast_multiply_fusion.8) | copy-start | bytes 1540
  9.5 88.7 %copy-start.29 = (f32[128]{0:T(128)}, f32[128]{0:T(128)S(1)}, u32[]{:S(2)}) copy-start(f32[128]{0:T(128)S(1)} %add_rsqrt_fusion.2) | copy-start | bytes 1540
  11.7 86.6 %all-gather.13.cloned.1.call-start = ((), (), s32[]{:S(2)}) async-start(), calls=%async_computation.11 | async-start | bytes 2228224 | tf_op jit(solution)/shard_map/all_gather | solution.py:275
  13.8 126.8 %all-gather.15.cloned.1.call-start = ((), (), s32[]{:S(2)}) async-start(), calls=%async_computation.12 | async-start | bytes 2228224 | tf_op jit(solution)/shard_map/all_gather | solution.py:295
  15.8 167.0 %all-gather.17.cloned.1.call-start = ((), (), s32[]{:S(2)}) async-start(), calls=%async_computation.13 | async-start | bytes 2228224 | tf_op jit(solution)/shard_map/all_gather | solution.py:296
  17.9 283.0 %all-gather.29.cloned.1.call-start = ((), (), s32[]{:S(2)}) async-start(), calls=%async_computation.19 | async-start | bytes 2228224 | tf_op jit(solution)/shard_map/all_gather | solution.py:365
  19.3 79.0 %copy-start.18 = (bf16[128,512]{1,0:T(8,128)(2,1)}, bf16[128,512]{1,0:T(8,128)(2,1)S(1)}, u32[]{:S(2)}) copy-start(bf16[128,512]{1,0:T(8,128)(2,1)S(1)} %fusion.68) | copy-start | bytes 393220
  20.9 77.4 %copy-start.39 = (s32[128]{0:T(128)}, s32[128]{0:T(128)S(1)}, u32[]{:S(2)}) copy-start(s32[128]{0:T(128)S(1)} %iota_add_fusion) | copy-start | bytes 1540
  21.0 77.2 %copy-start.40 = (s32[128]{0:T(128)}, s32[128]{0:T(128)S(1)}, u32[]{:S(2)}) copy-start(s32[128]{0:T(128)S(1)} %convert_reduce_fusion.10) | copy-start | bytes 1540
  98.2 26.1 %copy-start.5 = (bf16[1,128,512]{2,1,0:T(8,128)(2,1)S(1)}, bf16[1,128,512]{2,1,0:T(8,128)(2,1)}, u32[]{:S(2)}) copy-start(bf16[1,128,512]{2,1,0:T(8,128)(2,1)} %param.40) | copy-start | bytes 393220
  98.2 26.1 %copy-start.37 = (f32[512]{0:T(512)S(1)}, f32[512]{0:T(512)}, u32[]{:S(2)}) copy-start(f32[512]{0:T(512)} %param.52) | copy-start | bytes 6148
  98.2 27.7 %copy-start.22 = (f32[512]{0:T(512)S(1)}, f32[512]{0:T(512)}, u32[]{:S(2)}) copy-start(f32[512]{0:T(512)} %param.53) | copy-start | bytes 6148
  98.2 27.7 %copy-start.36 = (f32[512]{0:T(512)S(1)}, f32[512]{0:T(512)}, u32[]{:S(2)}) copy-start(f32[512]{0:T(512)} %param.54) | copy-start | bytes 6148
  98.2 27.7 %copy-start.38 = (f32[512]{0:T(512)S(1)}, f32[512]{0:T(512)}, u32[]{:S(2)}) copy-start(f32[512]{0:T(512)} %param.56) | copy-start | bytes 6148
  105.6 3.2 copy-start.1
  123.5 0.8 copy-start.27
  123.5 59.3 %copy-start.8 = (f32[8,128,64]{1,2,0:T(8,128)}, f32[8,128,64]{1,2,0:T(8,128)S(1)}, u32[]{:S(2)}) copy-start(f32[8,128,64]{1,2,0:T(8,128)S(1)} %get-tuple-element.163) | copy-start | bytes 786436
  124.3 1.6 copy-start.17
  125.7 57.1 %copy-start.32 = (f32[128]{0:T(128)}, f32[128]{0:T(128)S(1)}, u32[]{:S(2)}) copy-start(f32[128]{0:T(128)S(1)} %broadcast_multiply_fusion.7) | copy-start | bytes 1540
  126.0 56.9 %copy-start.35 = (f32[128]{0:T(128)}, f32[128]{0:T(128)S(1)}, u32[]{:S(2)}) copy-start(f32[128]{0:T(128)S(1)} %add_rsqrt_fusion.1) | copy-start | bytes 1540
  127.3 55.5 %copy-start.16 = (bf16[128,512]{1,0:T(8,128)(2,1)}, bf16[128,512]{1,0:T(8,128)(2,1)S(1)}, u32[]{:S(2)}) copy-start(bf16[128,512]{1,0:T(8,128)(2,1)S(1)} %fusion.70) | copy-start | bytes 393220
  182.8 28.6 %copy-start.23 = (f32[512]{0:T(512)S(1)}, f32[512]{0:T(512)}, u32[]{:S(2)}) copy-start(f32[512]{0:T(512)} %param.62) | copy-start | bytes 6148
  190.3 3.2 copy-start.2
  208.8 9.5 copy-start.9
  208.9 8.1 copy-start.6
  208.9 9.5 copy-start.19
  208.9 10.3 copy-start.11
  209.8 1.7 copy-start.15
  211.2 7.9 copy-start.31
  211.5 7.7 copy-start.34
  213.6 1.0 copy-start.3
  216.9 1.5 copy-start.12
  220.2 82.5 %all-gather.27.cloned.1.call-start = ((), (), s32[]{:S(2)}) async-start(), calls=%async_computation.18 | async-start | bytes 2228224 | tf_op jit(solution)/shard_map/all_gather | solution.py:364
  220.7 139.6 %all-gather.19.cloned.1.call-start = ((), (), s32[]{:S(2)}) async-start(), calls=%async_computation.14 | async-start | bytes 2228224 | tf_op jit(solution)/shard_map/all_gather | solution.py:425
  221.5 166.8 %all-gather.21.cloned.1.call-start = ((), (), s32[]{:S(2)}) async-start(), calls=%async_computation.15 | async-start | bytes 2228224 | tf_op jit(solution)/shard_map/all_gather | solution.py:426
  222.2 242.3 %all-gather.23.cloned.1.call-start = ((), (), s32[]{:S(2)}) async-start(), calls=%async_computation.16 | async-start | bytes 2228224 | tf_op jit(solution)/shard_map/all_gather | solution.py:421
  223.0 249.9 %all-gather.25.cloned.1.call-start = ((), (), s32[]{:S(2)}) async-start(), calls=%async_computation.17 | async-start | bytes 2228224 | tf_op jit(solution)/shard_map/all_gather | solution.py:422
  255.3 98.7 %copy-start.7 = (f32[128,512]{1,0:T(8,128)}, f32[128,512]{1,0:T(8,128)S(1)}, u32[]{:S(2)}) copy-start(f32[128,512]{1,0:T(8,128)S(1)} %get-tuple-element.490) | copy-start | bytes 786436
  257.5 343.5 %reduce-scatter.31.cloned.1.call-start = ((), (), s32[]{:S(2)}) async-start(), calls=%async_computation.28 | async-start | bytes 1114112
  339.6 9.8 copy-start.33
  339.6 17.8 %copy-start.28 = (f32[8,128]{1,0:T(8,128)S(1)}, f32[8,128]{1,0:T(8,128)}, u32[]{:S(2)}) copy-start(f32[8,128]{1,0:T(8,128)} %copy-done.27) | copy-start | bytes 12292
  344.4 258.2 %reduce-scatter.33.cloned.1.call-start = ((), (), s32[]{:S(2)}) async-start(), calls=%async_computation.29 | async-start | bytes 1114112
  349.3 304.1 %reduce-scatter.23.cloned.1.call-start = ((), (), s32[]{:S(2)}) async-start(), calls=%async_computation.24 | async-start | bytes 1114112 | tf_op jit(solution)/shard_map/reduce_scatter | solution.py:474
  351.8 362.0 %reduce-scatter.25.cloned.1.call-start = ((), (), s32[]{:S(2)}) async-start(), calls=%async_computation.25 | async-start | bytes 1114112 | tf_op jit(solution)/shard_map/reduce_scatter | solution.py:479
  354.0 419.7 %reduce-scatter.21.cloned.1.call-start = ((), (), s32[]{:S(2)}) async-start(), calls=%async_computation.23 | async-start | bytes 1114112 | tf_op jit(solution)/shard_map/reduce_scatter | solution.py:470
  356.4 477.7 %reduce-scatter.15.cloned.1.call-start = ((), (), s32[]{:S(2)}) async-start(), calls=%async_computation.20 | async-start | bytes 1114112 | tf_op jit(solution)/shard_map/reduce_scatter | solution.py:465
  388.3 35.5 %copy-start.21 = (f32[512]{0:T(512)S(1)}, f32[512]{0:T(512)}, u32[]{:S(2)}) copy-start(f32[512]{0:T(512)} %param.44) | copy-start | bytes 6148
  388.3 35.5 %copy-start.25 = (f32[128]{0:T(128)S(1)}, f32[128]{0:T(128)}, u32[]{:S(2)}) copy-start(f32[128]{0:T(128)} %copy-done.24) | copy-start | bytes 1540
  388.3 35.5 %copy-start.26 = (f32[512]{0:T(512)S(1)}, f32[512]{0:T(512)}, u32[]{:S(2)}) copy-start(f32[512]{0:T(512)} %param.45) | copy-start | bytes 6148
  388.3 84.5 %copy-start.13 = (bf16[128,512]{1,0:T(8,128)(2,1)S(1)}, bf16[128,512]{1,0:T(8,128)(2,1)}, u32[]{:S(2)}) copy-start(bf16[128,512]{1,0:T(8,128)(2,1)} %convolution_convert_fusion.3) | copy-start | bytes 393220
  388.3 84.5 %copy-start.14 = (bf16[128,512]{1,0:T(8,128)(2,1)S(1)}, bf16[128,512]{1,0:T(8,128)(2,1)}, u32[]{:S(2)}) copy-start(bf16[128,512]{1,0:T(8,128)(2,1)} %fusion.69) | copy-start | bytes 393220
  388.3 84.5 %copy-start.20 = (pred[2048,128]{1,0:T(8,128)(4,1)S(1)}, pred[2048,128]{1,0:T(8,128)(4,1)}, u32[]{:S(2)}) copy-start(pred[2048,128]{1,0:T(8,128)(4,1)} %get-tuple-element.496) | copy-start | bytes 786436
  423.8 49.1 %copy-start.10 = (bf16[128,8,64]{0,2,1:T(8,128)(2,1)}, bf16[128,8,64]{0,2,1:T(8,128)(2,1)S(1)}, u32[]{:S(2)}) copy-start(bf16[128,8,64]{0,2,1:T(8,128)(2,1)S(1)} %get-tuple-element.577) | copy-start | bytes 393220
  425.9 468.2 %reduce-scatter.17.cloned.1.call-start = ((), (), s32[]{:S(2)}) async-start(), calls=%async_computation.21 | async-start | bytes 1114112 | tf_op jit(solution)/shard_map/reduce_scatter | solution.py:467
  506.5 8.9 copy-start.4
  509.0 445.4 %reduce-scatter.19.cloned.1.call-start = ((), (), s32[]{:S(2)}) async-start(), calls=%async_computation.22 | async-start | bytes 1114112 | tf_op jit(solution)/shard_map/reduce_scatter | solution.py:468
  511.4 7.9 copy-start.41
  511.4 518.3 %reduce-scatter.27.cloned.1.call-start = ((), (), s32[]{:S(2)}) async-start(), calls=%async_computation.26 | async-start | bytes 4456448 | tf_op jit(solution)/shard_map/reduce_scatter | solution.py:483
  515.4 17.0 %copy-start.30 = (f32[128]{0:T(128)S(1)}, f32[128]{0:T(128)}, u32[]{:S(2)}) copy-start(f32[128]{0:T(128)} %copy-done.29) | copy-start | bytes 1540
  515.4 590.0 %reduce-scatter.29.cloned.1.call-start = ((), (), s32[]{:S(2)}) async-start(), calls=%async_computation.27 | async-start | bytes 4456448 | tf_op jit(solution)/shard_map/reduce_scatter | solution.py:485
  519.1 639.2 %all-reduce.19.cloned.1.call-start = ((), (), s32[]{:S(2)}) async-start(), calls=%async_computation.30 | async-start | bytes 2883584 | tf_op jit(solution)/shard_map/psum | solution.py:488
Sparse Core Ops, SparseCore 0:
  11.8 44.0 all-gather.10
  58.0 40.1 all-gather.12
  100.4 40.1 all-gather.14
  142.6 40.1 all-gather.16
  220.3 40.1 all-gather.28
  262.5 40.1 all-gather.26
  305.4 40.4 all-gather.18
  348.1 40.2 all-gather.20
  390.5 40.1 all-gather.22
  432.7 40.1 all-gather.24
  476.5 56.3 reduce-scatter.30
  536.8 56.4 reduce-scatter.32
  596.9 56.5 reduce-scatter.22
  657.3 56.4 reduce-scatter.24
  717.3 56.4 reduce-scatter.20
  777.6 56.4 reduce-scatter.14
  837.6 56.4 reduce-scatter.16
  898.0 56.3 reduce-scatter.18
  958.3 71.4 reduce-scatter.26
  1033.9 71.4 reduce-scatter.28
  1108.9 49.3 all-reduce.18
where the time goes:
time: 1190 us; the launch traced here: 1180 us
  waiting for transfers between devices  719 us (60%)
  matrix products  159 us (13%)
  blocking collectives  144 us (12%)
  local copies, waits for them, and re-layouts  93.8 us (8%)
  other arithmetic  31.7 us (3%)
  between operations  19.1 us (2%)
  loops' own time  13.2 us (1%)
    reduce_scatter x1, waiting for transfers between devices, local(): lax.psum_scatter(feed_parts[4], 'blk', scatter_dimension=0, tiled=True)  75.7 us
    reduce_scatter x1, waiting for transfers between devices, local(): lax.psum_scatter(feed_parts[2], 'blk', scatter_dimension=0, tiled=True)  75.3 us
    unnamed x1, blocking collectives  60.5 us
    reduce_scatter x1, waiting for transfers between devices, local(): lax.psum_scatter(self_parts[2], 'blk', scatter_dimension=0, tiled=True)  60.4 us
    reduce_scatter x1, waiting for transfers between devices, local(): lax.psum_scatter(cross_parts[7], 'blk', scatter_dimension=0, tiled=True)  60.4 us
    reduce_scatter x1, waiting for transfers between devices, local(): lax.psum_scatter(self_parts[5], 'blk', scatter_dimension=0, tiled=True)  60.3 us
    reduce_scatter x1, waiting for transfers between devices, local(): lax.psum_scatter(self_parts[4], 'blk', scatter_dimension=0, tiled=True)  60 us
    reduce_scatter x1, waiting for transfers between devices, local(): lax.psum_scatter(self_parts[7], 'blk', scatter_dimension=0, tiled=True)  59.9 us
  transfers between devices with their start and end apart: 21, of which 16 were waited for; matrix products, arithmetic and copies ran while one was open for 19% of the time, Pallas kernels for 0%

commit v1 on v0

--- a/solution.py
+++ b/solution.py
@@ -1,6 +1,11 @@
+import functools
+import typing
+
 import jax
 import jax.numpy as jnp
 from jax import lax
+from jax.experimental import pallas as pl
+from jax.experimental.pallas import tpu as pltpu
 from jax.sharding import PartitionSpec as P
 
 HEADS = 8
@@ -517,9 +522,820 @@
     return (layer_out[None], residues_grad[None], memory_grad[None]) + tuple(totals)
 
 
+BLOCK = 128
+HALF = 64
+CHIPS = 8
+HEAD = 64
+WIDE = 512
+HIDDEN = 2048
+ROUND = 16
+MASKED = -1e30
+ONES_LANE = 5
+SELF, CROSS = 0, 1
+MESH = pl.DeviceIdType.MESH
+VMEM = pl.BlockSpec(memory_space=pltpu.VMEM)
+SMEM = pl.BlockSpec(memory_space=pltpu.SMEM)
+PLACED = pl.BlockSpec(memory_space=pl.ANY)
+BF16, F32 = jnp.bfloat16, jnp.float32
+
+SQ, SK, SV, SO, CQ, CK, CV, CO = range(8)
+(
+    ROW_SELF_GAIN, ROW_SELF_SHIFT, ROW_SQ, ROW_SV, ROW_SO, ROW_CROSS_GAIN, ROW_CROSS_SHIFT, ROW_CQ, ROW_CV, ROW_CO,
+    ROW_FEED_GAIN, ROW_FEED_SHIFT, ROW_OUT, ROW_IN,
+) = range(14)
+VECTOR_ROWS = 24
+UNIT_OUT, UNIT_IN = 0, 4
+UNIT_OF = {CO: 8, CQ: 9, CK: 10, CV: 11, SO: 12, SQ: 13, SK: 14, SV: 15}
+UNITS = 16
+SPANS = ((0, 9), (9, 13), (13, 16))
+X_SQ, X_SO, X_CQ, X_CO, X_CDO, X_CDQ, X_SDO, X_SDQ = range(8)
+
+
+class Operands(typing.NamedTuple):
+    residues: VMEM
+    memory: VMEM
+    lengths: SMEM
+    cotangent: VMEM
+    self_norm_gain: VMEM
+    self_norm_bias: VMEM
+    self_query: PLACED
+    self_query_bias: VMEM
+    self_key: PLACED
+    self_value: PLACED
+    self_value_bias: VMEM
+    self_output: PLACED
+    self_output_bias: VMEM
+    cross_norm_gain: VMEM
+    cross_norm_bias: VMEM
+    cross_query: PLACED
+    cross_query_bias: VMEM
+    cross_key: PLACED
+    cross_value: PLACED
+    cross_value_bias: VMEM
+    cross_output: PLACED
+    cross_output_bias: VMEM
+    feed_norm_gain: VMEM
+    feed_norm_bias: VMEM
+    feed_in: PLACED
+    feed_in_bias: VMEM
+    feed_out: PLACED
+    feed_out_bias: VMEM
+
+
+AT_LAYER, AT_RESIDUES, AT_MEMORY, AT_SQUARE, AT_IN, AT_OUT, AT_VECTORS = 0, 128, 256, 384, 640, 768, 896
+RESULT_ROWS = AT_VECTORS + VECTOR_ROWS
+
+
+class Scratch(typing.NamedTuple):
+    final: pltpu.VMEM((RESULT_ROWS, WIDE), F32)
+    w_square: pltpu.VMEM((8, WIDE, WIDE), BF16)
+    w_in: pltpu.VMEM((WIDE, HIDDEN), BF16)
+    w_out: pltpu.VMEM((HIDDEN, WIDE), BF16)
+    kv_out: pltpu.VMEM((2, CHIPS, BLOCK, BLOCK), BF16)
+    kv: pltpu.VMEM((2, 2 * CHIPS, BLOCK, BLOCK), BF16)
+    narrow_out: pltpu.VMEM((8, CHIPS, HALF, BLOCK), BF16)
+    narrow: pltpu.VMEM((8, CHIPS, HALF, BLOCK), BF16)
+    dkv_out: pltpu.VMEM((2, CHIPS, BLOCK, BLOCK), BF16)
+    dkv: pltpu.VMEM((2, CHIPS, BLOCK, BLOCK), BF16)
+    dkv_part: pltpu.VMEM((2, CHIPS, 2, BLOCK, BLOCK), BF16)
+    dkv_other: pltpu.VMEM((2, CHIPS, BLOCK, BLOCK), BF16)
+    dkv_sum: pltpu.VMEM((2048, BLOCK), F32)
+    q_rows: pltpu.VMEM((2, 1024, BLOCK), BF16)
+    q_features: pltpu.VMEM((2, 1024, BLOCK), BF16)
+    do_rows: pltpu.VMEM((2, 1024, BLOCK), BF16)
+    o_rows: pltpu.VMEM((2, 1024, BLOCK), F32)
+    do_features: pltpu.VMEM((1024, BLOCK), BF16)
+    query_features: pltpu.VMEM((1024, BLOCK), BF16)
+    key_features: pltpu.VMEM((2048, BLOCK), BF16)
+    causal: pltpu.VMEM((256, 512), F32)
+    causal_turned: pltpu.VMEM((512, 256), F32)
+    scores: pltpu.VMEM((256, 2048), F32)
+    units: pltpu.VMEM((3, BLOCK, WIDE), F32)
+    factors: pltpu.VMEM((3, BLOCK, BLOCK), F32)
+    normed: pltpu.VMEM((3, BLOCK, WIDE), BF16)
+    attended: pltpu.VMEM((2, BLOCK, WIDE), BF16)
+    upstream: pltpu.VMEM((BLOCK, WIDE), F32)
+    grad_active: pltpu.VMEM((BLOCK, HIDDEN), F32)
+    active: pltpu.VMEM((BLOCK, HIDDEN), BF16)
+    grad_inner: pltpu.VMEM((BLOCK, HIDDEN), BF16)
+    parts: pltpu.VMEM((UNITS, 4, 2, 2, 2, ROUND, WIDE), BF16)
+    by_core: pltpu.VMEM((UNITS, 4, 2, 2, ROUND, WIDE), BF16)
+    by_side: pltpu.VMEM((UNITS, 4, 2, ROUND, WIDE), BF16)
+    by_column: pltpu.VMEM((UNITS, 4, ROUND, WIDE), BF16)
+    by_plane: pltpu.VMEM((3, UNITS, ROUND, WIDE), BF16)
+    halves: pltpu.VMEM((2, UNITS, ROUND, WIDE), BF16)
+    vectors: pltpu.VMEM((VECTOR_ROWS, WIDE), F32)
+    vec_in: pltpu.VMEM((3, VECTOR_ROWS, WIDE), F32)
+    vec_sum: pltpu.VMEM((2, VECTOR_ROWS, WIDE), F32)
+    vec_planes: pltpu.VMEM((4, VECTOR_ROWS, WIDE), F32)
+    load_sems: pltpu.SemaphoreType.DMA((10,))
+    narrow_sems: pltpu.SemaphoreType.DMA((2, 8, CHIPS))
+    kv_sems: pltpu.SemaphoreType.DMA((2, 2, CHIPS))
+    dkv_sems: pltpu.SemaphoreType.DMA((2, 2, CHIPS))
+    pass_sems: pltpu.SemaphoreType.DMA((2, 2, CHIPS))
+    share_sems: pltpu.SemaphoreType.DMA((2, 2))
+    reduce_sems: pltpu.SemaphoreType.DMA((2, 3, 7))
+    vec_sems: pltpu.SemaphoreType.DMA((2, 6))
+    final_sems: pltpu.SemaphoreType.DMA((16,))
+
+
+def specs_of(kind):
+    return tuple(kind.__annotations__.values())
+
+
+def dot_nn(left, right):
+    return lax.dot_general(left, right, (((1,), (0,)), ((), ())), preferred_element_type=F32)
+
+
+def dot_nt(left, right):
+    return lax.dot_general(left, right, (((1,), (1,)), ((), ())), preferred_element_type=F32)
+
+
+def dot_tn(left, right):
+    return lax.dot_general(left, right, (((0,), (0,)), ((), ())), preferred_element_type=F32)
+
+
+def low_lanes(shape):
+    return lax.broadcasted_iota(jnp.int32, shape, len(shape) - 1) < HEAD
+
+
+def turn(block):
+    return pltpu.roll(block, HEAD, 1)
+
+
+def swap(first, second):
+    keep = low_lanes(first.shape)
+    return jnp.where(keep, first, turn(second)), jnp.where(keep, turn(first), second)
+
+
+def column_sum(low):
+    return jnp.sum(low.astype(F32), 0, keepdims=True)
+
+
+def flat(ref):
+    return ref[...].reshape(1, -1)
+
+
+def fused_kernel(*refs):
+    count = len(specs_of(Operands))
+    a, result, s = Operands(*refs[:count]), refs[count], Scratch(*refs[count + 1 :])
+
+    rank = lax.axis_index("blk")
+    side = lax.axis_index("batch")
+    chip, core = lax.div(rank, 2), lax.rem(rank, 2)
+    plane, column = lax.div(chip, 2), lax.rem(chip, 2)
+
+    def around(shift):
+        return lax.rem(chip + (CHIPS + shift), CHIPS)
+
+    def at_rank(index):
+        return {"blk": index}
+
+    partner = at_rank(2 * chip + 1 - core)
+    beside = at_rank(2 * (2 * plane + 1 - column) + core)
+    across = {"batch": 1 - side}
+
+    def remote(src, dst, sems, device):
+        return pltpu.make_async_remote_copy(
+            src_ref=src, dst_ref=dst, send_sem=sems[0], recv_sem=sems[1], device_id=device, device_id_type=MESH
+        )
+
+    sent = []
+
+    def send(make, *which):
+        make(*which).start()
+        sent.append(functools.partial(make, *which))
+
+    finished = []
+
+    def final_put(at, values):
+        s.final[pl.ds(at, values.shape[0]), : values.shape[1]] = values
+
+    def final_start(at, rows):
+        span = pl.ds(at, rows)
+        finished.append(pltpu.make_async_copy(s.final.at[span], result.at[span], s.final_sems.at[len(finished)]))
+        finished[-1].start()
+
+    loads = {}
+    for at, (source, target) in enumerate(
+        (
+            (a.self_key, s.w_square.at[SK]), (a.self_value, s.w_square.at[SV]), (a.self_query, s.w_square.at[SQ]),
+            (a.cross_key, s.w_square.at[CK]), (a.cross_value, s.w_square.at[CV]), (a.feed_out, s.w_out),
+            (a.self_output, s.w_square.at[SO]), (a.cross_query, s.w_square.at[CQ]),
+            (a.cross_output, s.w_square.at[CO]), (a.feed_in, s.w_in),
+        )
+    ):
+        copy = pltpu.make_async_copy(source, target, s.load_sems.at[at])
+        copy.start()
+        loads[(SK, SV, SQ, CK, CV, 8, SO, CQ, CO, 9)[at]] = copy
+
+    def weight(which):
+        if which in loads:
+            loads.pop(which).wait()
+        return s.w_square[which] if which < 8 else (s.w_out, s.w_in)[which - 8]
+
+    barrier = pltpu.get_barrier_semaphore()
+    for shift in range(1, CHIPS):
+        pl.semaphore_signal(barrier, inc=1, device_id=at_rank(2 * around(shift) + core), device_id_type=MESH)
+    pl.semaphore_signal(barrier, inc=1, device_id=partner, device_id_type=MESH)
+    pl.semaphore_signal(barrier, inc=1, device_id=across, device_id_type=MESH)
+
+    class Exchange:
+        def __init__(self, outgoing, incoming, sems, which, by_token=False):
+            self.outgoing, self.incoming, self.by_token = outgoing.at[which], incoming.at[which], by_token
+            self.sems = lambda shift: (sems.at[0, which, shift], sems.at[1, which, shift])
+
+        def slot(self, source):
+            return self.incoming.at[2 * source + core if self.by_token else source]
+
+        def copy(self, shift):
+            to = around(shift)
+            return remote(self.outgoing.at[to], self.slot(chip), self.sems(shift), at_rank(2 * to + core))
+
+        def start(self):
+            for shift in range(1, CHIPS):
+                send(self.copy, shift)
+            self.slot(chip)[...] = self.outgoing[chip]
+
+        def wait(self, shift):
+            source = around(-shift)
+            remote(
+                self.outgoing.at[source], self.slot(source), self.sems(shift), at_rank(2 * source + core)
+            ).wait_recv()
+
+        def wait_all(self):
+            for shift in range(1, CHIPS):
+                self.wait(shift)
+
+    narrow = [Exchange(s.narrow_out, s.narrow, s.narrow_sems, which) for which in range(8)]
+    keys_values = [Exchange(s.kv_out, s.kv, s.kv_sems, which, True) for which in (SELF, CROSS)]
+    key_grads = [Exchange(s.dkv_out, s.dkv, s.dkv_sems, which) for which in (SELF, CROSS)]
+
+    def pass_copy(kind, shift, which_core):
+        slot = s.kv.at[kind, 2 * around(-shift) + which_core]
+        return remote(slot, slot, (s.pass_sems.at[0, kind, shift], s.pass_sems.at[1, kind, shift]), partner)
+
+    def pass_on(kind):
+        for shift in range(CHIPS):
+            if shift > 0:
+                keys_values[kind].wait(shift)
+            send(pass_copy, kind, shift, core)
+
+    def pass_wait(kind):
+        for shift in range(CHIPS):
+            pass_copy(kind, shift, 1 - core).wait_recv()
+
+    def pack_groups(matrix, which):
+        for pair in range(CHIPS // 2):
+            group = matrix[:, BLOCK * pair : BLOCK * (pair + 1)]
+            one, two = swap(group[:HALF], group[HALF:])
+            s.narrow_out[which, 2 * pair] = one.astype(BF16)
+            s.narrow_out[which, 2 * pair + 1] = two.astype(BF16)
+
+    def unpack_groups(which):
+        groups = []
+        for pair in range(CHIPS // 2):
+            groups.append(
+                jnp.concatenate(
+                    swap(s.narrow[which, 2 * pair].astype(F32), s.narrow[which, 2 * pair + 1].astype(F32)), 0
+                )
+            )
+        return jnp.concatenate(groups, 1).astype(BF16)
+
+    def pack_pairs(keys, values, kind):
+        for pair in range(CHIPS // 2):
+            lanes = slice(BLOCK * pair, BLOCK * (pair + 1))
+            one, two = swap(keys[:, lanes], values[:, lanes])
+            s.kv_out[kind, 2 * pair] = one.astype(BF16)
+            s.kv_out[kind, 2 * pair + 1] = two.astype(BF16)
+
+    def unpack_pairs(kind):
+        pairs = [
+            swap(s.dkv[kind, 2 * pair].astype(F32), s.dkv[kind, 2 * pair + 1].astype(F32)) for pair in range(CHIPS // 2)
+        ]
+        return tuple(jnp.concatenate(each, 1).astype(BF16) for each in zip(*pairs, strict=True))
+
+    def reduce_copy(stage, group):
+        first, last = SPANS[group]
+        span = pl.ds(first, last - first)
+        sems = (s.reduce_sems.at[0, group, stage], s.reduce_sems.at[1, group, stage])
+        if stage == 0:
+            return remote(s.parts.at[span, :, :, 1 - core], s.by_core.at[span], sems, partner)
+        if stage == 1:
+            return remote(s.by_core.at[span, :, :, 1 - side], s.by_side.at[span], sems, across)
+        if stage == 2:
+            return remote(s.by_side.at[span, :, 1 - column], s.by_column.at[span], sems, beside)
+        if stage < 6:
+            to = lax.rem(plane + (stage - 2), 4)
+            return remote(
+                s.by_column.at[span, to], s.by_plane.at[stage - 3, span], sems, at_rank(2 * (2 * to + column) + core)
+            )
+        return remote(s.halves.at[side, span], s.halves.at[side, span], sems, across)
+
+    def reduce_start(stage, group):
+        for each in (3, 4, 5) if stage == 3 else (stage,):
+            send(reduce_copy, each, group)
+
+    def reduce_finish(stage, group):
+        first, last = SPANS[group]
+        for each in (3, 4, 5) if stage == 3 else (stage,):
+            if each == 6:
+                half = s.halves.at[1 - side, pl.ds(first, last - first)]
+                remote(half, half, (s.reduce_sems.at[0, group, 6], s.reduce_sems.at[1, group, 6]), across).wait_recv()
+            else:
+                reduce_copy(each, group).wait_recv()
+
+        def add(unit, nothing):
+            if stage == 0:
+                s.by_core[unit] = s.by_core[unit] + s.parts[unit, :, :, core]
+            if stage == 1:
+                s.by_side[unit] = s.by_side[unit] + s.by_core[unit, :, :, side]
+            if stage == 2:
+                s.by_column[unit] = s.by_column[unit] + s.by_side[unit, :, column]
+            if stage == 3:
+                total = s.by_column[unit, plane].astype(F32)
+                for each in range(3):
+                    total = total + s.by_plane[each, unit].astype(F32)
+                s.halves[side, unit] = total.astype(BF16)
+            return nothing
+
+        if stage < 6:
+            lax.fori_loop(first, last, add, 0)
+
+    def reduce_step(stage, group):
+        reduce_finish(stage, group)
+        reduce_start(stage + 1 if stage < 3 else 6, group)
+
+    def put_unit(unit, value):
+        s.parts[unit] = value.astype(BF16).reshape(4, 2, 2, 2, ROUND, WIDE)
+
+    def put_vector(row, values):
+        for piece in range(values.shape[1] // WIDE):
+            s.vectors[pl.ds(row + piece, 1), :] = values[:, piece * WIDE : (piece + 1) * WIDE]
+
+    def norm(values, which, gain, shift):
+        average = jnp.mean(values, -1, keepdims=True)
+        centred = values - average
+        factor = lax.rsqrt(jnp.mean(centred * centred, -1, keepdims=True) + EPS)
+        normal = centred * factor
+        s.units[which] = normal
+        s.factors[which] = jnp.broadcast_to(factor, (BLOCK, BLOCK))
+        low = (normal * flat(gain) + flat(shift)).astype(BF16)
+        s.normed[which] = low
+        return low
+
+    def norm_gradient(gradient, which, gain, row):
+        normal = s.units[which]
+        weighted = gradient * flat(gain)
+        one = jnp.mean(weighted, -1, keepdims=True)
+        two = jnp.mean(weighted * normal, -1, keepdims=True)
+        put_vector(row, jnp.sum(gradient * normal, 0, keepdims=True))
+        put_vector(row + 1, jnp.sum(gradient, 0, keepdims=True))
+        return s.factors[which][:, :1] * (weighted - one - normal * two)
+
+    def query_rows(which, target, low_half):
+        keep = low_lanes((HALF, BLOCK))
+
+        def one(block, nothing):
+            piece = s.narrow[which, block].astype(F32)
+            rolled = turn(piece)
+            if low_half:
+                top, bottom = jnp.where(keep, piece, 0.0), jnp.where(keep, rolled, 0.0)
+            else:
+                top, bottom = jnp.where(keep, 0.0, rolled), jnp.where(keep, 0.0, piece)
+            target[pl.ds(block * BLOCK, BLOCK), :] = jnp.concatenate([top, bottom], 0).astype(BF16)
+            return nothing
+
+        lax.fori_loop(0, CHIPS, one, 0)
+
+    def key_block(kind, chunk):
+        rows = s.kv[kind, pl.ds(4 * chunk, 4)].reshape(512, BLOCK)
+        return jnp.concatenate([rows, s.key_features[pl.ds(512 * chunk, 512), :]], 1)
+
+    def with_column(features, column_values):
+        lane = lax.broadcasted_iota(jnp.int32, features.shape, 1)
+        full = jnp.broadcast_to(column_values, features.shape)
+        high = full.astype(BF16).astype(F32)
+        middle = (full - high).astype(BF16).astype(F32)
+        low = full - high - middle
+        for at, piece in enumerate((high, middle, low)):
+            features = jnp.where(lane == ONES_LANE + at, piece, features)
+        return features.astype(BF16)
+
+    def attend(kind, causal, which):
+        def part_of(part, pieces):
+            rows = pl.ds(part * 256, 256)
+            queries = jnp.concatenate([s.q_rows[kind, rows, :], s.query_features[rows, :]], 1)
+            highest = None
+            for chunk in range(pieces):
+                scores = dot_nt(queries, key_block(kind, chunk))
+                if causal and chunk == pieces - 1:
+                    scores = scores + s.causal[...]
+                s.scores[:, 512 * chunk : 512 * (chunk + 1)] = scores
+                for at in range(4):
+                    piece = scores[:, BLOCK * at : BLOCK * (at + 1)]
+                    highest = piece if highest is None else jnp.maximum(highest, piece)
+            highest = jnp.max(highest, 1, keepdims=True)
+            summed = None
+            for chunk in range(pieces):
+                weights = jnp.exp(s.scores[:, 512 * chunk : 512 * (chunk + 1)] - highest).astype(BF16)
+                piece = dot_nn(weights, key_block(kind, chunk))
+                summed = piece if summed is None else summed + piece
+            total = summed[:, BLOCK + ONES_LANE : BLOCK + ONES_LANE + 1]
+            result = summed[:, :BLOCK] / total
+            s.o_rows[kind, rows, :] = result
+            s.q_features[kind, rows, :] = with_column(
+                s.query_features[rows, :].astype(F32), -(highest + jnp.log(total))
+            )
+            keep = low_lanes((HALF, BLOCK))
+            for half in range(2):
+                block = result[BLOCK * half : BLOCK * (half + 1)]
+                s.narrow_out[which, 2 * part + half] = jnp.where(keep, turn(block[:HALF]), block[HALF:]).astype(BF16)
+
+        if causal:
+            for part in range(4):
+                part_of(part, part + 1)
+        else:
+
+            def loop(part, nothing):
+                part_of(part, 4)
+                return nothing
+
+            lax.fori_loop(0, 4, loop, 0)
+
+    def attend_back(kind, causal, which_in, which_out):
+        query_rows(which_in, s.do_rows.at[kind], False)
+
+        def spreads(part, nothing):
+            rows = pl.ds(part * 256, 256)
+            spread = jnp.sum(s.do_rows[kind, rows, :].astype(F32) * s.o_rows[kind, rows, :], 1, keepdims=True)
+            s.do_features[rows, :] = with_column(jnp.zeros((256, BLOCK), F32), -spread)
+            return nothing
+
+        lax.fori_loop(0, 4, spreads, 0)
+
+        def one(part, chunk, diagonal):
+            rows = pl.ds(part * 256, 256)
+            keys = key_block(kind, chunk)
+            queries, grads = s.q_rows[kind, rows, :], s.do_rows[kind, rows, :]
+            scores = dot_nt(keys, jnp.concatenate([queries, s.q_features[kind, rows, :]], 1))
+            if diagonal:
+                scores = scores + s.causal_turned[...]
+            weights = jnp.exp(scores)
+            slopes = dot_nt(keys, jnp.concatenate([grads, s.do_features[rows, :]], 1))
+            tilted = (weights * slopes).astype(BF16)
+            shares = dot_nn(tilted, queries) + dot_nn(weights.astype(BF16), grads)
+            return shares, dot_tn(tilted, keys[:, :BLOCK])
+
+        def part_of(part, pieces):
+            total = None
+            for chunk in range(pieces):
+                shares, toward = one(part, chunk, causal and chunk == pieces - 1)
+                where = pl.ds(512 * chunk, 512)
+                if causal and part == chunk:
+                    s.dkv_sum[where, :] = shares
+                else:
+                    s.dkv_sum[where, :] = s.dkv_sum[where, :] + shares
+                total = toward if total is None else total + toward
+            total = total * (HEAD**-0.5)
+            keep = low_lanes((HALF, BLOCK))
+            for half in range(2):
+                block = total[BLOCK * half : BLOCK * (half + 1)]
+                s.narrow_out[which_out, 2 * part + half] = jnp.where(keep, block[:HALF], turn(block[HALF:])).astype(
+                    BF16
+                )
+
+        if causal:
+            for part in range(4):
+                part_of(part, part + 1)
+        else:
+            s.dkv_sum[...] = jnp.zeros(s.dkv_sum.shape, F32)
+
+            def loop(part, nothing):
+                part_of(part, 4)
+                return nothing
+
+            lax.fori_loop(0, 4, loop, 0)
+        s.dkv_part[kind] = s.dkv_sum[...].astype(BF16).reshape(CHIPS, 2, BLOCK, BLOCK)
+
+    def share_copy(kind):
+        return remote(
+            s.dkv_part.at[kind, :, 1 - core], s.dkv_other.at[kind], (s.share_sems.at[0, kind], s.share_sems.at[1, kind]),
+            partner,
+        )
+
+    def share_finish(kind):
+        share_copy(kind).wait_recv()
+        s.dkv_out[kind] = s.dkv_part[kind, :, core] + s.dkv_other[kind]
+
+    inputs = a.residues[...].astype(F32)
+    normed = norm(inputs, 0, a.self_norm_gain, a.self_norm_bias)
+    keys = dot_nn(normed, weight(SK))
+    values = dot_nn(normed, weight(SV)) + flat(a.self_value_bias)
+    pack_pairs(keys, values, SELF)
+    pl.semaphore_wait(barrier, CHIPS + 1)
+    keys_values[SELF].start()
+    queries = (dot_nn(normed, weight(SQ)) + flat(a.self_query_bias)) * (HEAD**-0.5)
+    pack_groups(queries, X_SQ)
+    narrow[X_SQ].start()
+
+    encoded = a.memory[...]
+    keys = dot_nn(encoded, weight(CK))
+    values = dot_nn(encoded, weight(CV)) + flat(a.cross_value_bias)
+    pack_pairs(keys, values, CROSS)
+
+    bounds, reach = [], 0
+    for at in range(4):
+        reach = reach + a.lengths[0, at]
+        bounds.append(reach)
+    lane = lax.broadcasted_iota(jnp.int32, (BLOCK, BLOCK), 1)
+    row = lax.broadcasted_iota(jnp.int32, (BLOCK, BLOCK), 0)
+
+    def documents(position):
+        found = jnp.zeros((BLOCK, BLOCK), jnp.int32)
+        for bound in bounds:
+            found = found + (position >= bound).astype(jnp.int32)
+        return found
+
+    ones = jnp.where((lane >= ONES_LANE) & (lane < ONES_LANE + 3), 1.0, 0.0)
+
+    def key_features(block, nothing):
+        other = documents(row + block * BLOCK) != lane
+        s.key_features[pl.ds(block * BLOCK, BLOCK), :] = jnp.where((lane < ONES_LANE) & other, MASKED, ones).astype(
+            BF16
+        )
+        return nothing
+
+    lax.fori_loop(0, 2 * CHIPS, key_features, 0)
+
+    def query_features(block, nothing):
+        same = documents(row + (2 * block + core) * BLOCK) == lane
+        s.query_features[pl.ds(block * BLOCK, BLOCK), :] = jnp.where((lane < ONES_LANE) & same, 1.0, 0.0).astype(BF16)
+        return nothing
+
+    lax.fori_loop(0, CHIPS, query_features, 0)
+
+    def query_place(at):
+        return at + core * BLOCK + jnp.where(at >= BLOCK, BLOCK, 0)
+
+    at_row = lax.broadcasted_iota(jnp.int32, (256, 512), 0)
+    at_key = lax.broadcasted_iota(jnp.int32, (256, 512), 1)
+    s.causal[...] = jnp.where(at_key <= query_place(at_row), 0.0, MASKED)
+    at_key = lax.broadcasted_iota(jnp.int32, (512, 256), 0)
+    at_row = lax.broadcasted_iota(jnp.int32, (512, 256), 1)
+    s.causal_turned[...] = jnp.where(at_key <= query_place(at_row), 0.0, MASKED)
+    pass_on(SELF)
+    keys_values[CROSS].start()
+    narrow[X_SQ].wait_all()
+    query_rows(X_SQ, s.q_rows.at[SELF], True)
+    pass_wait(SELF)
+    attend(SELF, True, X_SO)
+    narrow[X_SO].start()
+    grads = a.cotangent[...]
+    weight(8)
+    for piece in range(4):
+        lanes = slice(512 * piece, 512 * (piece + 1))
+        s.grad_active[:, lanes] = dot_nt(grads, s.w_out[lanes, :])
+    pass_on(CROSS)
+    narrow[X_SO].wait_all()
+    self_low = unpack_groups(X_SO)
+    s.attended[SELF] = self_low
+    after_self = inputs + dot_nn(self_low, weight(SO)) + flat(a.self_output_bias)
+
+    normed = norm(after_self, 1, a.cross_norm_gain, a.cross_norm_bias)
+    queries = (dot_nn(normed, weight(CQ)) + flat(a.cross_query_bias)) * (HEAD**-0.5)
+    pack_groups(queries, X_CQ)
+    narrow[X_CQ].start()
+    pass_wait(CROSS)
+    narrow[X_CQ].wait_all()
+    query_rows(X_CQ, s.q_rows.at[CROSS], True)
+    attend(CROSS, False, X_CO)
+    narrow[X_CO].start()
+    weight(9)
+    narrow[X_CO].wait_all()
+    cross_low = unpack_groups(X_CO)
+    s.attended[CROSS] = cross_low
+    after_cross = after_self + dot_nn(cross_low, weight(CO)) + flat(a.cross_output_bias)
+
+    normed = norm(after_cross, 2, a.feed_norm_gain, a.feed_norm_bias)
+    layer_out, back = after_cross + flat(a.feed_out_bias), None
+    for piece in range(4):
+        lanes = slice(512 * piece, 512 * (piece + 1))
+        inner = dot_nn(normed, s.w_in[:, lanes]) + flat(a.feed_in_bias)[:, lanes]
+        bell = 0.5 * (1.0 + lax.erf(inner * SQRT_HALF))
+        active = (inner * bell).astype(BF16)
+        slope = bell + inner * jnp.exp(-0.5 * inner * inner) * INV_ROOT_TAU
+        grad_inner = (s.grad_active[:, lanes] * slope).astype(BF16)
+        s.active[:, lanes] = active
+        s.grad_inner[:, lanes] = grad_inner
+        layer_out = layer_out + dot_nn(active, s.w_out[lanes, :])
+        toward = dot_nt(grad_inner, s.w_in[:, lanes])
+        back = toward if back is None else back + toward
+    final_put(AT_LAYER, layer_out)
+    final_start(AT_LAYER, BLOCK)
+    upstream = a.cotangent[...].astype(F32)
+    upstream = upstream + norm_gradient(back, 2, a.feed_norm_gain, ROW_FEED_GAIN)
+
+    branch = upstream.astype(BF16)
+    pack_groups(dot_nt(branch, weight(CO)), X_CDO)
+    narrow[X_CDO].start()
+    s.upstream[...] = upstream
+    put_vector(ROW_OUT, column_sum(a.cotangent[...]))
+    put_vector(ROW_IN, column_sum(s.grad_inner[...]))
+    put_vector(ROW_CO, column_sum(branch))
+    for piece in range(4):
+        lanes = slice(512 * piece, 512 * (piece + 1))
+        part = dot_tn(s.active[:, lanes], a.cotangent[...]).astype(BF16).reshape(2, 2, 4, 2, ROUND, WIDE)
+        for each in range(4):
+            s.parts[UNIT_OUT + each, piece] = part[:, :, each]
+        put_unit(UNIT_IN + piece, dot_tn(s.normed[2], s.grad_inner[:, lanes]))
+    put_unit(UNIT_OF[CO], dot_tn(s.attended[CROSS], branch))
+    reduce_start(0, 0)
+    narrow[X_CDO].wait_all()
+    attend_back(CROSS, False, X_CDO, X_CDQ)
+    narrow[X_CDQ].start()
+    send(share_copy, CROSS)
+    reduce_step(0, 0)
+    share_finish(CROSS)
+    key_grads[CROSS].start()
+    narrow[X_CDQ].wait_all()
+    grad_query = unpack_groups(X_CDQ)
+    gradient = dot_nt(grad_query, weight(CQ))
+    upstream = s.upstream[...] + norm_gradient(gradient, 1, a.cross_norm_gain, ROW_CROSS_GAIN)
+
+    branch = upstream.astype(BF16)
+    pack_groups(dot_nt(branch, weight(SO)), X_SDO)
+    narrow[X_SDO].start()
+    s.upstream[...] = upstream
+    put_vector(ROW_SO, column_sum(branch))
+    put_vector(ROW_CQ, column_sum(grad_query))
+    put_unit(UNIT_OF[SO], dot_tn(s.attended[SELF], branch))
+    put_unit(UNIT_OF[CQ], dot_tn(s.normed[1], grad_query))
+    key_grads[CROSS].wait_all()
+    grad_key, grad_value = unpack_pairs(CROSS)
+    put_vector(ROW_CV, column_sum(grad_value))
+    put_unit(UNIT_OF[CK], dot_tn(a.memory[...], grad_key))
+    put_unit(UNIT_OF[CV], dot_tn(a.memory[...], grad_value))
+    reduce_start(0, 1)
+    final_put(AT_MEMORY, dot_nt(grad_key, weight(CK)) + dot_nt(grad_value, weight(CV)))
+    final_start(AT_MEMORY, BLOCK)
+    narrow[X_SDO].wait_all()
+    attend_back(SELF, True, X_SDO, X_SDQ)
+    narrow[X_SDQ].start()
+    send(share_copy, SELF)
+    reduce_step(1, 0)
+    reduce_step(0, 1)
+    share_finish(SELF)
+    key_grads[SELF].start()
+    narrow[X_SDQ].wait_all()
+    grad_query = unpack_groups(X_SDQ)
+    key_grads[SELF].wait_all()
+    grad_key, grad_value = unpack_pairs(SELF)
+    normed = s.normed[0]
+    put_unit(UNIT_OF[SQ], dot_tn(normed, grad_query))
+    put_unit(UNIT_OF[SK], dot_tn(normed, grad_key))
+    put_unit(UNIT_OF[SV], dot_tn(normed, grad_value))
+    reduce_start(0, 2)
+    put_vector(ROW_SQ, column_sum(grad_query))
+    put_vector(ROW_SV, column_sum(grad_value))
+    gradient = dot_nt(grad_query, weight(SQ)) + dot_nt(grad_key, weight(SK)) + dot_nt(grad_value, weight(SV))
+    final_put(AT_RESIDUES, s.upstream[...] + norm_gradient(gradient, 0, a.self_norm_gain, ROW_SELF_GAIN))
+    final_start(AT_RESIDUES, BLOCK)
+
+    def vector_copy(stage):
+        sems = (s.vec_sems.at[0, stage], s.vec_sems.at[1, stage])
+        if stage == 0:
+            return remote(s.vectors, s.vec_in.at[0], sems, partner)
+        if stage == 1:
+            return remote(s.vec_sum.at[0], s.vec_in.at[1], sems, across)
+        if stage == 2:
+            return remote(s.vec_sum.at[1], s.vec_in.at[2], sems, beside)
+        to = lax.rem(plane + (stage - 2), 4)
+        return remote(s.vec_planes.at[plane], s.vec_planes.at[plane], sems, at_rank(2 * (2 * to + column) + core))
+
+    s.vectors[pl.ds(17, VECTOR_ROWS - 17), :] = jnp.zeros((VECTOR_ROWS - 17, WIDE), F32)
+    send(vector_copy, 0)
+    reduce_step(2, 0)
+    reduce_step(1, 1)
+    vector_copy(0).wait_recv()
+    s.vec_sum[0] = s.vectors[...] + s.vec_in[0]
+    send(vector_copy, 1)
+    reduce_step(0, 2)
+    reduce_step(3, 0)
+    reduce_step(2, 1)
+    vector_copy(1).wait_recv()
+    s.vec_sum[1] = s.vec_sum[0] + s.vec_in[1]
+    send(vector_copy, 2)
+    reduce_step(1, 2)
+    vector_copy(2).wait_recv()
+    s.vec_planes[plane] = s.vec_sum[1] + s.vec_in[2]
+    for stage in (3, 4, 5):
+        send(vector_copy, stage)
+    reduce_step(3, 1)
+    reduce_step(2, 2)
+    reduce_finish(6, 0)
+    for stage in (3, 4, 5):
+        source = lax.rem(plane + 4 - (stage - 2), 4)
+        remote(
+            s.vec_planes.at[plane], s.vec_planes.at[source], (s.vec_sems.at[0, stage], s.vec_sems.at[1, stage]), beside
+        ).wait_recv()
+    total = s.vec_planes[0]
+    for each in range(1, 4):
+        total = total + s.vec_planes[each]
+    shares = pltpu.roll(total, lax.rem(WIDE - 32 * rank, WIDE), 1)[:, :BLOCK]
+    turned = pltpu.roll(total, lax.rem(WIDE - BLOCK * lax.rem(rank, 4), WIDE), 1)[:, :BLOCK]
+    own = jnp.zeros((1, BLOCK), F32)
+    for each in range(4):
+        own = own + jnp.where(lax.div(rank, 4) == each, turned[ROW_IN + each : ROW_IN + each + 1], 0.0)
+    s.final[pl.ds(AT_VECTORS, VECTOR_ROWS), :BLOCK] = shares
+    s.final[pl.ds(AT_VECTORS + ROW_IN, 1), :BLOCK] = own
+    final_start(AT_VECTORS, VECTOR_ROWS)
+
+    def unit_value(unit):
+        return jnp.concatenate([s.halves[0, unit], s.halves[1, unit]], 0).astype(F32)
+
+    def put_final_unit(at, unit):
+        final_put(at, unit_value(unit))
+
+    for piece in range(4):
+        put_final_unit(AT_OUT + 32 * piece, UNIT_OUT + piece)
+        put_final_unit(AT_IN + 32 * piece, UNIT_IN + piece)
+    final_start(AT_IN, 2 * BLOCK)
+    reduce_step(3, 2)
+    reduce_finish(6, 1)
+    for which in (CO, CQ, CK, CV, SO):
+        put_final_unit(AT_SQUARE + 32 * which, UNIT_OF[which])
+    reduce_finish(6, 2)
+    for which in (SQ, SK, SV):
+        put_final_unit(AT_SQUARE + 32 * which, UNIT_OF[which])
+    final_start(AT_SQUARE, 256)
+    for copy in finished:
+        copy.wait()
+    for make in sent:
+        make().wait_send()
+
+
+def place_kernel(packed, *refs):
+    results, vectors, sems = refs[:-2], refs[-2], refs[-1]
+    copies = []
+
+    def place(at, target):
+        source = packed.at[pl.ds(at, target.shape[0]), pl.ds(0, target.shape[1])]
+        copies.append(pltpu.make_async_copy(source, target, sems.at[len(copies)]))
+        copies[-1].start()
+
+    place(AT_VECTORS, vectors)
+    for at, target in zip((AT_LAYER, AT_RESIDUES, AT_MEMORY), results[:3], strict=True):
+        place(at, target)
+    for which, at in SQUARE_RESULTS.items():
+        place(AT_SQUARE + 32 * which, results[at])
+    for piece in range(4):
+        place(AT_IN + 32 * piece, results[23].at[:, pl.ds(512 * piece, 512)])
+    place(AT_OUT, results[25])
+    copies[0].wait()
+    rows = vectors[...]
+    for row, at in VECTOR_RESULTS.items():
+        results[at][...] = rows[row, : results[at].shape[0]]
+    for copy in copies[1:]:
+        copy.wait()
+
+
+SQUARE_RESULTS = {SQ: 5, SK: 7, SV: 8, SO: 10, CQ: 14, CK: 16, CV: 17, CO: 19}
+VECTOR_RESULTS = {
+    ROW_SELF_GAIN: 3, ROW_SELF_SHIFT: 4, ROW_SQ: 6, ROW_SV: 9, ROW_SO: 11, ROW_CROSS_GAIN: 12, ROW_CROSS_SHIFT: 13,
+    ROW_CQ: 15, ROW_CV: 18, ROW_CO: 20, ROW_FEED_GAIN: 21, ROW_FEED_SHIFT: 22, ROW_OUT: 26, ROW_IN: 24,
+}
+
+
+def fused(residues, memory, lengths, cotangent, *parameters):
+    packed = pl.pallas_call(
+        fused_kernel,
+        out_shape=jax.ShapeDtypeStruct((RESULT_ROWS, WIDE), F32),
+        in_specs=specs_of(Operands),
+        out_specs=PLACED,
+        scratch_shapes=specs_of(Scratch),
+        compiler_params=pltpu.CompilerParams(
+            collective_id=0, has_side_effects=True, vmem_limit_bytes=60 * 1024 * 1024
+        ),
+    )(residues[0], memory[0], lengths, cotangent[0], *parameters)
+    shapes = [jax.ShapeDtypeStruct((BLOCK, WIDE), F32)] * 3
+    for parameter in parameters:
+        shapes.append(jax.ShapeDtypeStruct((parameter.shape[0] // (2 * CHIPS),) + parameter.shape[1:], F32))
+    results = pl.pallas_call(
+        place_kernel,
+        out_shape=shapes,
+        in_specs=(PLACED,),
+        out_specs=(VMEM,) * len(shapes),
+        scratch_shapes=(pltpu.VMEM((VECTOR_ROWS, BLOCK), F32), pltpu.SemaphoreType.DMA((17,))),
+        compiler_params=pltpu.CompilerParams(vmem_limit_bytes=60 * 1024 * 1024),
+    )(packed)
+    return tuple(each[None] for each in results[:3]) + tuple(results[3:])
+
+
 def solution(mesh):
+    fits = mesh.shape["blk"] == 2 * CHIPS and mesh.shape["batch"] == 2
     return jax.shard_map(
-        local,
+        fused if fits else local,
         mesh=mesh,
         in_specs=(
             P("batch", "blk", None),

time: 1190 us -> 138 us (0.12)
  waiting for transfers between devices: 719 us -> 0 us
  matrix products: 159 us -> 0 us
  blocking collectives: 144 us -> 0 us
  Pallas kernels: 0 us -> 137 us
  local copies, waits for them, and re-layouts: 93.8 us -> 0 us
  other arithmetic: 31.7 us -> 0 us
  between operations: 19.1 us -> 0.85 us
  loops' own time: 13.2 us -> 0 us
    reduce_scatter x8 -> x0, waiting for transfers between devices: 501 us -> none  [the longest x1 75.7 us: local(): lax.psum_scatter(feed_parts[4], 'blk', scatter_dimension=0, tiled=True)]
    all_gather x10 -> x0, waiting for transfers between devices: 168 us -> none  [the longest x1 42.4 us: local(): lax.all_gather(self_v, 'blk', axis=0, tiled=True)]
    dot_general x44 -> x0, matrix products: 159 us -> none  [the longest x2 22.6 us: active(): jnp.einsum('hqk,qhd->khd', tilted, query_heads, preferred_element_type=jn...]
    pallas_call x0 -> x2, Pallas kernels: none -> 137 us  [the longest x1 134 us: fused(): pl.pallas_call(fused_kernel, out_shape=jax.ShapeDtypeStruct((RESULT_ROWS,...]
    all_gather x4 -> x0, blocking collectives: 78.1 us -> none  [the longest x2 40.6 us: local(): lax.all_gather(spread, 'blk', axis=0, tiled=True)]
    unnamed x1 -> x0, blocking collectives: 60.5 us -> none
    another operation x16 -> x0, local copies, waits for them, and re-layouts: 51.1 us -> none
    psum x1 -> x0, waiting for transfers between devices: 47.5 us -> none  [local(): lax.psum((ordered[0], ordered[1], ordered[2], ordered[3], ordered[4], ord...]
  transfers between devices with their start and end apart: 21 -> 0, of which waited for: 16 -> 0; matrix products, arithmetic and copies ran while one was open for 19% -> 0% of each run, Pallas kernels for 0% -> 0%
where the time goes in v1:
time: 138 us
  Pallas kernels  137 us (99%)
    pallas_call x1, Pallas kernels, fused(): pl.pallas_call(fused_kernel, out_shape=jax.ShapeDtypeStruct((RESULT_ROWS,...  134 us
    pallas_call x1, Pallas kernels, fused(): pl.pallas_call(place_kernel, out_shape=shapes, in_specs=(PLACED,), out_sp...  2.87 us

profile of v1, /device:TPU:0, one launch (start us, length us, event | category | flops | bytes accessed | tf_op | source)
XLA Modules:
  0.0 137.9 jit_solution(3080993094114122296)
XLA Ops:
  0.7 134.1 %shard_map.475.packed = f32[920,512]{1,0:T(8,128)} custom-call(bf16[128,512]{1,0:T(8,128)(2,1)} %bitcast.6, bf16[128,512]{1,0:T(8,128)(2,1)} %bitcast.7, s32[1,4]{1,0:T(1,128)} %refs_2_.1, bf16[128,512]{1,0:T(8,128)(2,1)} %bitcast.8, f32[512]{0:T(512)} %refs_4_.1, f32[512]{0:T(512)} %refs_5_.1, bf16[512,512]{1,0:T(8,128)(2,1)} %refs_6_.1, f32[512]{0:T(512)} %refs_7_.1, ...), custom_call_target="tpu_custom_call" | custom-call | tf_op jit(solution)/shard_map/pallas_call | solution.py:1311
  134.8 2.9 %shard_map.476 = (f32[128,512]{1,0:T(8,128)}, f32[128,512]{1,0:T(8,128)}, f32[128,512]{1,0:T(8,128)}, f32[32]{0:T(128)}, f32[32]{0:T(128)}, /*index=5*/f32[32,51...) custom-call(f32[920,512]{1,0:T(8,128)} %shard_map.475.packed), custom_call_target="tpu_custom_call" | custom-call | tf_op jit(solution)/shard_map/pallas_call | solution.py:1324

commit v2 on v1

--- a/solution.py
+++ b/solution.py
@@ -1,4 +1,3 @@
-import functools
 import typing
 
 import jax
@@ -545,9 +544,11 @@
 ) = range(14)
 VECTOR_ROWS = 24
 UNIT_OUT, UNIT_IN = 0, 4
-UNIT_OF = {CO: 8, CQ: 9, CK: 10, CV: 11, SO: 12, SQ: 13, SK: 14, SV: 15}
+UNIT_OF = {CO: 8, SO: 9, CQ: 10, CK: 11, CV: 12, SQ: 13, SV: 14, SK: 15}
 UNITS = 16
-SPANS = ((0, 9), (9, 13), (13, 16))
+G_OUT, G_MORE, G_IN, G_REST, G_EARLY, G_CROSS, G_SELF, G_LAST = range(8)
+SPANS = ((0, 2), (2, 4), (4, 6), (6, 9), (9, 11), (11, 13), (13, 15), (15, 16))
+COLUMN_FIRST = (G_OUT, G_LAST)
 X_SQ, X_SO, X_CQ, X_CO, X_CDO, X_CDQ, X_SDO, X_SDQ = range(8)
 
 
@@ -599,7 +600,7 @@
     dkv: pltpu.VMEM((2, CHIPS, BLOCK, BLOCK), BF16)
     dkv_part: pltpu.VMEM((2, CHIPS, 2, BLOCK, BLOCK), BF16)
     dkv_other: pltpu.VMEM((2, CHIPS, BLOCK, BLOCK), BF16)
-    dkv_sum: pltpu.VMEM((2048, BLOCK), F32)
+    dq_turned: pltpu.VMEM((BLOCK, 1024), F32)
     q_rows: pltpu.VMEM((2, 1024, BLOCK), BF16)
     q_features: pltpu.VMEM((2, 1024, BLOCK), BF16)
     do_rows: pltpu.VMEM((2, 1024, BLOCK), BF16)
@@ -609,7 +610,6 @@
     key_features: pltpu.VMEM((2048, BLOCK), BF16)
     causal: pltpu.VMEM((256, 512), F32)
     causal_turned: pltpu.VMEM((512, 256), F32)
-    scores: pltpu.VMEM((256, 2048), F32)
     units: pltpu.VMEM((3, BLOCK, WIDE), F32)
     factors: pltpu.VMEM((3, BLOCK, BLOCK), F32)
     normed: pltpu.VMEM((3, BLOCK, WIDE), BF16)
@@ -625,18 +625,19 @@
     by_plane: pltpu.VMEM((3, UNITS, ROUND, WIDE), BF16)
     halves: pltpu.VMEM((2, UNITS, ROUND, WIDE), BF16)
     vectors: pltpu.VMEM((VECTOR_ROWS, WIDE), F32)
-    vec_in: pltpu.VMEM((3, VECTOR_ROWS, WIDE), F32)
-    vec_sum: pltpu.VMEM((2, VECTOR_ROWS, WIDE), F32)
-    vec_planes: pltpu.VMEM((4, VECTOR_ROWS, WIDE), F32)
+    vec_in: pltpu.VMEM((CHIPS, VECTOR_ROWS, BLOCK), F32)
+    vec_four: pltpu.VMEM((4, VECTOR_ROWS, BLOCK), F32)
     load_sems: pltpu.SemaphoreType.DMA((10,))
-    narrow_sems: pltpu.SemaphoreType.DMA((2, 8, CHIPS))
-    kv_sems: pltpu.SemaphoreType.DMA((2, 2, CHIPS))
-    dkv_sems: pltpu.SemaphoreType.DMA((2, 2, CHIPS))
-    pass_sems: pltpu.SemaphoreType.DMA((2, 2, CHIPS))
+    narrow_sems: pltpu.SemaphoreType.DMA((8,))
+    kv_sems: pltpu.SemaphoreType.DMA((2, CHIPS))
+    dkv_sems: pltpu.SemaphoreType.DMA((2,))
+    pass_sems: pltpu.SemaphoreType.DMA((2,))
     share_sems: pltpu.SemaphoreType.DMA((2, 2))
-    reduce_sems: pltpu.SemaphoreType.DMA((2, 3, 7))
-    vec_sems: pltpu.SemaphoreType.DMA((2, 6))
-    final_sems: pltpu.SemaphoreType.DMA((16,))
+    sent_sems: pltpu.SemaphoreType.DMA((7,))
+    reduce_sems: pltpu.SemaphoreType.DMA((len(SPANS), 5))
+    reduce_sent: pltpu.SemaphoreType.DMA((len(SPANS),))
+    vec_sems: pltpu.SemaphoreType.DMA((2,))
+    final_sems: pltpu.SemaphoreType.DMA((6,))
 
 
 def specs_of(kind):
@@ -694,17 +695,16 @@
     partner = at_rank(2 * chip + 1 - core)
     beside = at_rank(2 * (2 * plane + 1 - column) + core)
     across = {"batch": 1 - side}
+    opposite = {"blk": 2 * chip + 1 - core, "batch": 1 - side}
 
     def remote(src, dst, sems, device):
         return pltpu.make_async_remote_copy(
             src_ref=src, dst_ref=dst, send_sem=sems[0], recv_sem=sems[1], device_id=device, device_id_type=MESH
         )
 
-    sent = []
-
-    def send(make, *which):
-        make(*which).start()
-        sent.append(functools.partial(make, *which))
+    SENT_NARROW, SENT_KV, SENT_PASS, SENT_DKV, SENT_SHARE, SENT_VECTOR, SENT_FOUR = (
+        s.sent_sems.at[which] for which in range(7)
+    )
 
     finished = []
 
@@ -717,17 +717,14 @@
         finished[-1].start()
 
     loads = {}
-    for at, (source, target) in enumerate(
-        (
-            (a.self_key, s.w_square.at[SK]), (a.self_value, s.w_square.at[SV]), (a.self_query, s.w_square.at[SQ]),
-            (a.cross_key, s.w_square.at[CK]), (a.cross_value, s.w_square.at[CV]), (a.feed_out, s.w_out),
-            (a.self_output, s.w_square.at[SO]), (a.cross_query, s.w_square.at[CQ]),
-            (a.cross_output, s.w_square.at[CO]), (a.feed_in, s.w_in),
-        )
-    ):
-        copy = pltpu.make_async_copy(source, target, s.load_sems.at[at])
-        copy.start()
-        loads[(SK, SV, SQ, CK, CV, 8, SO, CQ, CO, 9)[at]] = copy
+
+    def load(*pairs):
+        for which, source in pairs:
+            target = s.w_square.at[which] if which < 8 else (s.w_out, s.w_in)[which - 8]
+            loads[which] = pltpu.make_async_copy(source, target, s.load_sems.at[which])
+            loads[which].start()
+
+    load((SK, a.self_key), (SV, a.self_value), (SQ, a.self_query))
 
     def weight(which):
         if which in loads:
@@ -737,53 +734,50 @@
     barrier = pltpu.get_barrier_semaphore()
     for shift in range(1, CHIPS):
         pl.semaphore_signal(barrier, inc=1, device_id=at_rank(2 * around(shift) + core), device_id_type=MESH)
-    pl.semaphore_signal(barrier, inc=1, device_id=partner, device_id_type=MESH)
-    pl.semaphore_signal(barrier, inc=1, device_id=across, device_id_type=MESH)
+    for other in (partner, across, opposite):
+        pl.semaphore_signal(barrier, inc=1, device_id=other, device_id_type=MESH)
 
     class Exchange:
-        def __init__(self, outgoing, incoming, sems, which, by_token=False):
-            self.outgoing, self.incoming, self.by_token = outgoing.at[which], incoming.at[which], by_token
-            self.sems = lambda shift: (sems.at[0, which, shift], sems.at[1, which, shift])
+        def __init__(self, outgoing, incoming, sems, sent, which, by_source=False):
+            self.outgoing, self.incoming, self.by_source = outgoing.at[which], incoming.at[which], by_source
+            self.sems, self.sent = sems.at[which], sent
 
         def slot(self, source):
-            return self.incoming.at[2 * source + core if self.by_token else source]
-
-        def copy(self, shift):
-            to = around(shift)
-            return remote(self.outgoing.at[to], self.slot(chip), self.sems(shift), at_rank(2 * to + core))
+            return self.incoming.at[2 * source + core if self.by_source else source]
+
+        def pair(self, source):
+            return (self.sent, self.sems.at[source] if self.by_source else self.sems)
 
         def start(self):
             for shift in range(1, CHIPS):
-                send(self.copy, shift)
+                to = around(shift)
+                remote(self.outgoing.at[to], self.slot(chip), self.pair(chip), at_rank(2 * to + core)).start()
             self.slot(chip)[...] = self.outgoing[chip]
 
         def wait(self, shift):
             source = around(-shift)
             remote(
-                self.outgoing.at[source], self.slot(source), self.sems(shift), at_rank(2 * source + core)
+                self.outgoing.at[source], self.slot(source), self.pair(source), at_rank(2 * source + core)
             ).wait_recv()
 
         def wait_all(self):
-            for shift in range(1, CHIPS):
-                self.wait(shift)
-
-    narrow = [Exchange(s.narrow_out, s.narrow, s.narrow_sems, which) for which in range(8)]
-    keys_values = [Exchange(s.kv_out, s.kv, s.kv_sems, which, True) for which in (SELF, CROSS)]
-    key_grads = [Exchange(s.dkv_out, s.dkv, s.dkv_sems, which) for which in (SELF, CROSS)]
-
-    def pass_copy(kind, shift, which_core):
-        slot = s.kv.at[kind, 2 * around(-shift) + which_core]
-        return remote(slot, slot, (s.pass_sems.at[0, kind, shift], s.pass_sems.at[1, kind, shift]), partner)
+            seven = pl.ds(0, CHIPS - 1)
+            remote(self.outgoing.at[seven], self.incoming.at[seven], (self.sent, self.sems), partner).wait_recv()
+
+    narrow = [Exchange(s.narrow_out, s.narrow, s.narrow_sems, SENT_NARROW, which) for which in range(8)]
+    keys_values = [Exchange(s.kv_out, s.kv, s.kv_sems, SENT_KV, which, True) for which in (SELF, CROSS)]
+    key_grads = [Exchange(s.dkv_out, s.dkv, s.dkv_sems, SENT_DKV, which) for which in (SELF, CROSS)]
 
     def pass_on(kind):
         for shift in range(CHIPS):
             if shift > 0:
                 keys_values[kind].wait(shift)
-            send(pass_copy, kind, shift, core)
+            slot = s.kv.at[kind, 2 * around(-shift) + core]
+            remote(slot, slot, (SENT_PASS, s.pass_sems.at[kind]), partner).start()
 
     def pass_wait(kind):
-        for shift in range(CHIPS):
-            pass_copy(kind, shift, 1 - core).wait_recv()
+        eight = s.kv.at[kind, pl.ds(0, CHIPS)]
+        remote(eight, eight, (SENT_PASS, s.pass_sems.at[kind]), partner).wait_recv()
 
     def pack_groups(matrix, which):
         for pair in range(CHIPS // 2):
@@ -818,13 +812,16 @@
     def reduce_copy(stage, group):
         first, last = SPANS[group]
         span = pl.ds(first, last - first)
-        sems = (s.reduce_sems.at[0, group, stage], s.reduce_sems.at[1, group, stage])
+        sems = (s.reduce_sent.at[group], s.reduce_sems.at[group, {0: 0, 1: 1, 2: 2, 6: 4}.get(stage, 3)])
         if stage == 0:
             return remote(s.parts.at[span, :, :, 1 - core], s.by_core.at[span], sems, partner)
+        columns = (stage == 1) == (group in COLUMN_FIRST)
         if stage == 1:
-            return remote(s.by_core.at[span, :, :, 1 - side], s.by_side.at[span], sems, across)
+            source = s.by_core.at[span, :, 1 - column] if columns else s.by_core.at[span, :, :, 1 - side]
+            return remote(source, s.by_side.at[span], sems, beside if columns else across)
         if stage == 2:
-            return remote(s.by_side.at[span, :, 1 - column], s.by_column.at[span], sems, beside)
+            source = s.by_side.at[span, :, 1 - column if columns else 1 - side]
+            return remote(source, s.by_column.at[span], sems, beside if columns else across)
         if stage < 6:
             to = lax.rem(plane + (stage - 2), 4)
             return remote(
@@ -832,26 +829,38 @@
             )
         return remote(s.halves.at[side, span], s.halves.at[side, span], sems, across)
 
+    def planes_copy(group):
+        span = s.by_plane.at[:, pl.ds(SPANS[group][0], SPANS[group][1] - SPANS[group][0])]
+        return remote(span, span, (s.reduce_sent.at[group], s.reduce_sems.at[group, 3]), partner)
+
+    def reduce_sent(stage, group):
+        (planes_copy(group) if stage == 3 else reduce_copy(stage, group)).wait_send()
+
     def reduce_start(stage, group):
+        if stage > 0:
+            reduce_sent(3 if stage == 6 else stage - 1, group)
         for each in (3, 4, 5) if stage == 3 else (stage,):
-            send(reduce_copy, each, group)
+            reduce_copy(each, group).start()
 
     def reduce_finish(stage, group):
         first, last = SPANS[group]
-        for each in (3, 4, 5) if stage == 3 else (stage,):
-            if each == 6:
-                half = s.halves.at[1 - side, pl.ds(first, last - first)]
-                remote(half, half, (s.reduce_sems.at[0, group, 6], s.reduce_sems.at[1, group, 6]), across).wait_recv()
-            else:
-                reduce_copy(each, group).wait_recv()
+        if stage == 3:
+            planes_copy(group).wait_recv()
+        elif stage == 6:
+            half = s.halves.at[1 - side, pl.ds(first, last - first)]
+            remote(half, half, (s.reduce_sent.at[group], s.reduce_sems.at[group, 4]), across).wait_recv()
+        else:
+            reduce_copy(stage, group).wait_recv()
 
         def add(unit, nothing):
             if stage == 0:
                 s.by_core[unit] = s.by_core[unit] + s.parts[unit, :, :, core]
+            columns = (stage == 1) == (group in COLUMN_FIRST)
             if stage == 1:
-                s.by_side[unit] = s.by_side[unit] + s.by_core[unit, :, :, side]
+                own = s.by_core[unit, :, column] if columns else s.by_core[unit, :, :, side]
+                s.by_side[unit] = s.by_side[unit] + own
             if stage == 2:
-                s.by_column[unit] = s.by_column[unit] + s.by_side[unit, :, column]
+                s.by_column[unit] = s.by_column[unit] + s.by_side[unit, :, column if columns else side]
             if stage == 3:
                 total = s.by_column[unit, plane].astype(F32)
                 for each in range(3):
@@ -870,8 +879,14 @@
         s.parts[unit] = value.astype(BF16).reshape(4, 2, 2, 2, ROUND, WIDE)
 
     def put_vector(row, values):
-        for piece in range(values.shape[1] // WIDE):
-            s.vectors[pl.ds(row + piece, 1), :] = values[:, piece * WIDE : (piece + 1) * WIDE]
+        if values.shape[1] == WIDE:
+            s.vectors[pl.ds(row, 1), :] = values
+            return
+        for at in range(HIDDEN // BLOCK):
+            group, piece = divmod(at, 4)
+            s.vectors[pl.ds(row + piece, 1), BLOCK * group : BLOCK * (group + 1)] = values[
+                :, BLOCK * at : BLOCK * (at + 1)
+            ]
 
     def norm(values, which, gain, shift):
         average = jnp.mean(values, -1, keepdims=True)
@@ -893,20 +908,12 @@
         put_vector(row + 1, jnp.sum(gradient, 0, keepdims=True))
         return s.factors[which][:, :1] * (weighted - one - normal * two)
 
-    def query_rows(which, target, low_half):
+    def query_rows(kind, which):
         keep = low_lanes((HALF, BLOCK))
-
-        def one(block, nothing):
+        for block in range(CHIPS):
             piece = s.narrow[which, block].astype(F32)
-            rolled = turn(piece)
-            if low_half:
-                top, bottom = jnp.where(keep, piece, 0.0), jnp.where(keep, rolled, 0.0)
-            else:
-                top, bottom = jnp.where(keep, 0.0, rolled), jnp.where(keep, 0.0, piece)
-            target[pl.ds(block * BLOCK, BLOCK), :] = jnp.concatenate([top, bottom], 0).astype(BF16)
-            return nothing
-
-        lax.fori_loop(0, CHIPS, one, 0)
+            both = jnp.concatenate([jnp.where(keep, piece, 0.0), jnp.where(keep, turn(piece), 0.0)], 0)
+            s.q_rows[kind, pl.ds(block * BLOCK, BLOCK), :] = both.astype(BF16)
 
     def key_block(kind, chunk):
         rows = s.kv[kind, pl.ds(4 * chunk, 4)].reshape(512, BLOCK)
@@ -923,24 +930,26 @@
         return features.astype(BF16)
 
     def attend(kind, causal, which):
-        def part_of(part, pieces):
+        for part in range(4):
             rows = pl.ds(part * 256, 256)
             queries = jnp.concatenate([s.q_rows[kind, rows, :], s.query_features[rows, :]], 1)
-            highest = None
-            for chunk in range(pieces):
-                scores = dot_nt(queries, key_block(kind, chunk))
-                if causal and chunk == pieces - 1:
+            highest, summed = None, None
+            chunks = range(part, -1, -1) if causal else range(4)
+            for chunk in chunks:
+                keys = key_block(kind, chunk)
+                scores = dot_nt(queries, keys)
+                if causal and chunk == part:
                     scores = scores + s.causal[...]
-                s.scores[:, 512 * chunk : 512 * (chunk + 1)] = scores
-                for at in range(4):
-                    piece = scores[:, BLOCK * at : BLOCK * (at + 1)]
-                    highest = piece if highest is None else jnp.maximum(highest, piece)
-            highest = jnp.max(highest, 1, keepdims=True)
-            summed = None
-            for chunk in range(pieces):
-                weights = jnp.exp(s.scores[:, 512 * chunk : 512 * (chunk + 1)] - highest).astype(BF16)
-                piece = dot_nn(weights, key_block(kind, chunk))
-                summed = piece if summed is None else summed + piece
+                reach = scores[:, :BLOCK]
+                for at in range(1, 4):
+                    reach = jnp.maximum(reach, scores[:, BLOCK * at : BLOCK * (at + 1)])
+                reach = jnp.max(reach, 1, keepdims=True)
+                if summed is None:
+                    summed = dot_nn(jnp.exp(scores - reach).astype(BF16), keys)
+                else:
+                    reach = jnp.maximum(highest, reach)
+                    summed = summed * jnp.exp(highest - reach) + dot_nn(jnp.exp(scores - reach).astype(BF16), keys)
+                highest = reach
             total = summed[:, BLOCK + ONES_LANE : BLOCK + ONES_LANE + 1]
             result = summed[:, :BLOCK] / total
             s.o_rows[kind, rows, :] = result
@@ -952,89 +961,65 @@
                 block = result[BLOCK * half : BLOCK * (half + 1)]
                 s.narrow_out[which, 2 * part + half] = jnp.where(keep, turn(block[:HALF]), block[HALF:]).astype(BF16)
 
-        if causal:
-            for part in range(4):
-                part_of(part, part + 1)
-        else:
-
-            def loop(part, nothing):
-                part_of(part, 4)
-                return nothing
-
-            lax.fori_loop(0, 4, loop, 0)
-
-    def attend_back(kind, causal, which_in, which_out):
-        query_rows(which_in, s.do_rows.at[kind], False)
-
-        def spreads(part, nothing):
-            rows = pl.ds(part * 256, 256)
-            spread = jnp.sum(s.do_rows[kind, rows, :].astype(F32) * s.o_rows[kind, rows, :], 1, keepdims=True)
-            s.do_features[rows, :] = with_column(jnp.zeros((256, BLOCK), F32), -spread)
-            return nothing
-
-        lax.fori_loop(0, 4, spreads, 0)
-
-        def one(part, chunk, diagonal):
-            rows = pl.ds(part * 256, 256)
+    def attend_back(kind, causal, which_in, which_out, between):
+        keep = low_lanes((HALF, BLOCK))
+        for block in range(CHIPS):
+            rows = pl.ds(block * BLOCK, BLOCK)
+            piece = s.narrow[which_in, block].astype(F32)
+            gradient = jnp.concatenate([jnp.where(keep, 0.0, turn(piece)), jnp.where(keep, 0.0, piece)], 0)
+            s.do_rows[kind, rows, :] = gradient.astype(BF16)
+            spread = jnp.sum(gradient * s.o_rows[kind, rows, :], 1, keepdims=True)
+            s.do_features[rows, :] = with_column(jnp.zeros((BLOCK, BLOCK), F32), -spread)
+        for chunk in range(4):
             keys = key_block(kind, chunk)
-            queries, grads = s.q_rows[kind, rows, :], s.do_rows[kind, rows, :]
-            scores = dot_nt(keys, jnp.concatenate([queries, s.q_features[kind, rows, :]], 1))
-            if diagonal:
-                scores = scores + s.causal_turned[...]
-            weights = jnp.exp(scores)
-            slopes = dot_nt(keys, jnp.concatenate([grads, s.do_features[rows, :]], 1))
-            tilted = (weights * slopes).astype(BF16)
-            shares = dot_nn(tilted, queries) + dot_nn(weights.astype(BF16), grads)
-            return shares, dot_tn(tilted, keys[:, :BLOCK])
-
-        def part_of(part, pieces):
             total = None
-            for chunk in range(pieces):
-                shares, toward = one(part, chunk, causal and chunk == pieces - 1)
-                where = pl.ds(512 * chunk, 512)
+            for part in range(chunk if causal else 0, 4):
+                rows = pl.ds(part * 256, 256)
+                queries, grads = s.q_rows[kind, rows, :], s.do_rows[kind, rows, :]
+                scores = dot_nt(keys, jnp.concatenate([queries, s.q_features[kind, rows, :]], 1))
                 if causal and part == chunk:
-                    s.dkv_sum[where, :] = shares
-                else:
-                    s.dkv_sum[where, :] = s.dkv_sum[where, :] + shares
-                total = toward if total is None else total + toward
-            total = total * (HEAD**-0.5)
-            keep = low_lanes((HALF, BLOCK))
-            for half in range(2):
-                block = total[BLOCK * half : BLOCK * (half + 1)]
-                s.narrow_out[which_out, 2 * part + half] = jnp.where(keep, block[:HALF], turn(block[HALF:])).astype(
-                    BF16
+                    scores = scores + s.causal_turned[...]
+                weights = jnp.exp(scores)
+                slopes = dot_nt(keys, jnp.concatenate([grads, s.do_features[rows, :]], 1))
+                tilted = (weights * slopes).astype(BF16)
+                shares = dot_nn(
+                    jnp.concatenate([tilted, weights.astype(BF16)], 1), jnp.concatenate([queries, grads], 0)
                 )
-
-        if causal:
-            for part in range(4):
-                part_of(part, part + 1)
-        else:
-            s.dkv_sum[...] = jnp.zeros(s.dkv_sum.shape, F32)
-
-            def loop(part, nothing):
-                part_of(part, 4)
-                return nothing
-
-            lax.fori_loop(0, 4, loop, 0)
-        s.dkv_part[kind] = s.dkv_sum[...].astype(BF16).reshape(CHIPS, 2, BLOCK, BLOCK)
-
-    def share_copy(kind):
+                total = shares if total is None else total + shares
+                toward = dot_tn(keys[:, :BLOCK], tilted)
+                s.dq_turned[:, rows] = toward if chunk == 0 else s.dq_turned[:, rows] + toward
+            s.dkv_part[kind, 2 * chunk : 2 * chunk + 2] = total.astype(BF16).reshape(2, 2, BLOCK, BLOCK)
+            between(chunk)
+        for block in range(CHIPS):
+            s.narrow_out[which_out, block] = (
+                s.dq_turned[:HEAD, BLOCK * block : BLOCK * (block + 1)] * (HEAD**-0.5)
+            ).astype(BF16)
+
+    def turned_rows(which):
+        return s.narrow[which].reshape(WIDE, BLOCK).astype(F32).T.astype(BF16)
+
+    def share_copy(kind, part):
+        chips = pl.ds(4 * part, 4)
         return remote(
-            s.dkv_part.at[kind, :, 1 - core], s.dkv_other.at[kind], (s.share_sems.at[0, kind], s.share_sems.at[1, kind]),
+            s.dkv_part.at[kind, chips, 1 - core], s.dkv_other.at[kind, chips], (SENT_SHARE, s.share_sems.at[kind, part]),
             partner,
         )
 
     def share_finish(kind):
-        share_copy(kind).wait_recv()
-        s.dkv_out[kind] = s.dkv_part[kind, :, core] + s.dkv_other[kind]
+        for part in range(2):
+            share_copy(kind, part).wait_recv()
+            chips = slice(4 * part, 4 * part + 4)
+            s.dkv_out[kind, chips] = s.dkv_part[kind, chips, core] + s.dkv_other[kind, chips]
 
     inputs = a.residues[...].astype(F32)
     normed = norm(inputs, 0, a.self_norm_gain, a.self_norm_bias)
     keys = dot_nn(normed, weight(SK))
     values = dot_nn(normed, weight(SV)) + flat(a.self_value_bias)
     pack_pairs(keys, values, SELF)
-    pl.semaphore_wait(barrier, CHIPS + 1)
+    pl.semaphore_wait(barrier, CHIPS + 2)
     keys_values[SELF].start()
+    load((CK, a.cross_key), (CV, a.cross_value), (8, a.feed_out), (SO, a.self_output))
+    load((CQ, a.cross_query), (CO, a.cross_output), (9, a.feed_in))
     queries = (dot_nn(normed, weight(SQ)) + flat(a.self_query_bias)) * (HEAD**-0.5)
     pack_groups(queries, X_SQ)
     narrow[X_SQ].start()
@@ -1087,7 +1072,7 @@
     pass_on(SELF)
     keys_values[CROSS].start()
     narrow[X_SQ].wait_all()
-    query_rows(X_SQ, s.q_rows.at[SELF], True)
+    query_rows(SELF, X_SQ)
     pass_wait(SELF)
     attend(SELF, True, X_SO)
     narrow[X_SO].start()
@@ -1108,7 +1093,7 @@
     narrow[X_CQ].start()
     pass_wait(CROSS)
     narrow[X_CQ].wait_all()
-    query_rows(X_CQ, s.q_rows.at[CROSS], True)
+    query_rows(CROSS, X_CQ)
     attend(CROSS, False, X_CO)
     narrow[X_CO].start()
     weight(9)
@@ -1148,106 +1133,132 @@
         part = dot_tn(s.active[:, lanes], a.cotangent[...]).astype(BF16).reshape(2, 2, 4, 2, ROUND, WIDE)
         for each in range(4):
             s.parts[UNIT_OUT + each, piece] = part[:, :, each]
+    reduce_start(0, G_OUT)
+    reduce_start(0, G_MORE)
+    for piece in range(4):
+        lanes = slice(512 * piece, 512 * (piece + 1))
         put_unit(UNIT_IN + piece, dot_tn(s.normed[2], s.grad_inner[:, lanes]))
+        if piece == 1:
+            reduce_start(0, G_IN)
     put_unit(UNIT_OF[CO], dot_tn(s.attended[CROSS], branch))
-    reduce_start(0, 0)
+    reduce_start(0, G_REST)
+    reduce_step(0, G_MORE)
     narrow[X_CDO].wait_all()
-    attend_back(CROSS, False, X_CDO, X_CDQ)
+    reduce_step(0, G_OUT)
+
+    def between_cross(chunk):
+        if chunk == 0:
+            reduce_step(0, G_IN)
+        if chunk in (1, 3):
+            share_copy(CROSS, chunk // 2).start()
+
+    attend_back(CROSS, False, X_CDO, X_CDQ, between_cross)
     narrow[X_CDQ].start()
-    send(share_copy, CROSS)
-    reduce_step(0, 0)
     share_finish(CROSS)
     key_grads[CROSS].start()
+    reduce_step(1, G_OUT)
+    reduce_step(0, G_REST)
+    reduce_step(1, G_MORE)
     narrow[X_CDQ].wait_all()
-    grad_query = unpack_groups(X_CDQ)
+    grad_query = turned_rows(X_CDQ)
     gradient = dot_nt(grad_query, weight(CQ))
     upstream = s.upstream[...] + norm_gradient(gradient, 1, a.cross_norm_gain, ROW_CROSS_GAIN)
 
     branch = upstream.astype(BF16)
     pack_groups(dot_nt(branch, weight(SO)), X_SDO)
     narrow[X_SDO].start()
+    reduce_step(2, G_OUT)
+    reduce_step(1, G_IN)
     s.upstream[...] = upstream
     put_vector(ROW_SO, column_sum(branch))
     put_vector(ROW_CQ, column_sum(grad_query))
     put_unit(UNIT_OF[SO], dot_tn(s.attended[SELF], branch))
     put_unit(UNIT_OF[CQ], dot_tn(s.normed[1], grad_query))
+    reduce_start(0, G_EARLY)
     key_grads[CROSS].wait_all()
     grad_key, grad_value = unpack_pairs(CROSS)
     put_vector(ROW_CV, column_sum(grad_value))
     put_unit(UNIT_OF[CK], dot_tn(a.memory[...], grad_key))
     put_unit(UNIT_OF[CV], dot_tn(a.memory[...], grad_value))
-    reduce_start(0, 1)
+    reduce_start(0, G_CROSS)
+    reduce_step(0, G_EARLY)
     final_put(AT_MEMORY, dot_nt(grad_key, weight(CK)) + dot_nt(grad_value, weight(CV)))
     final_start(AT_MEMORY, BLOCK)
     narrow[X_SDO].wait_all()
-    attend_back(SELF, True, X_SDO, X_SDQ)
+    reduce_step(2, G_MORE)
+    reduce_step(1, G_REST)
+
+    def between_self(chunk):
+        if chunk == 0:
+            reduce_step(0, G_CROSS)
+        if chunk in (1, 3):
+            share_copy(SELF, chunk // 2).start()
+
+    attend_back(SELF, True, X_SDO, X_SDQ, between_self)
     narrow[X_SDQ].start()
-    send(share_copy, SELF)
-    reduce_step(1, 0)
-    reduce_step(0, 1)
     share_finish(SELF)
     key_grads[SELF].start()
+    reduce_step(3, G_OUT)
     narrow[X_SDQ].wait_all()
-    grad_query = unpack_groups(X_SDQ)
+    grad_query = turned_rows(X_SDQ)
+    put_unit(UNIT_OF[SQ], dot_tn(s.normed[0], grad_query))
+    reduce_step(1, G_EARLY)
     key_grads[SELF].wait_all()
     grad_key, grad_value = unpack_pairs(SELF)
     normed = s.normed[0]
-    put_unit(UNIT_OF[SQ], dot_tn(normed, grad_query))
+    put_unit(UNIT_OF[SV], dot_tn(normed, grad_value))
+    reduce_start(0, G_SELF)
     put_unit(UNIT_OF[SK], dot_tn(normed, grad_key))
-    put_unit(UNIT_OF[SV], dot_tn(normed, grad_value))
-    reduce_start(0, 2)
+    reduce_start(0, G_LAST)
     put_vector(ROW_SQ, column_sum(grad_query))
     put_vector(ROW_SV, column_sum(grad_value))
     gradient = dot_nt(grad_query, weight(SQ)) + dot_nt(grad_key, weight(SK)) + dot_nt(grad_value, weight(SV))
     final_put(AT_RESIDUES, s.upstream[...] + norm_gradient(gradient, 0, a.self_norm_gain, ROW_SELF_GAIN))
     final_start(AT_RESIDUES, BLOCK)
 
-    def vector_copy(stage):
-        sems = (s.vec_sems.at[0, stage], s.vec_sems.at[1, stage])
-        if stage == 0:
-            return remote(s.vectors, s.vec_in.at[0], sems, partner)
-        if stage == 1:
-            return remote(s.vec_sum.at[0], s.vec_in.at[1], sems, across)
-        if stage == 2:
-            return remote(s.vec_sum.at[1], s.vec_in.at[2], sems, beside)
-        to = lax.rem(plane + (stage - 2), 4)
-        return remote(s.vec_planes.at[plane], s.vec_planes.at[plane], sems, at_rank(2 * (2 * to + column) + core))
+    def vector_copy(shift):
+        if shift < CHIPS:
+            to = around(shift)
+            lanes = pl.ds(pl.multiple_of(lax.div(to, 2) * BLOCK, BLOCK), BLOCK)
+            sems = (SENT_VECTOR, s.vec_sems.at[0])
+            return remote(s.vectors.at[:, lanes], s.vec_in.at[shift], sems, at_rank(2 * to + core))
+        other = (partner, across, opposite)[shift - CHIPS]
+        return remote(s.vec_four.at[0], s.vec_four.at[shift - CHIPS + 1], (SENT_FOUR, s.vec_sems.at[1]), other)
+
+    def vector_all(step):
+        rows = s.vec_in.at[pl.ds(1, 7)] if step == 0 else s.vec_four.at[pl.ds(1, 3)]
+        return remote(rows, rows, ((SENT_VECTOR, SENT_FOUR)[step], s.vec_sems.at[step]), partner)
 
     s.vectors[pl.ds(17, VECTOR_ROWS - 17), :] = jnp.zeros((VECTOR_ROWS - 17, WIDE), F32)
-    send(vector_copy, 0)
-    reduce_step(2, 0)
-    reduce_step(1, 1)
-    vector_copy(0).wait_recv()
-    s.vec_sum[0] = s.vectors[...] + s.vec_in[0]
-    send(vector_copy, 1)
-    reduce_step(0, 2)
-    reduce_step(3, 0)
-    reduce_step(2, 1)
-    vector_copy(1).wait_recv()
-    s.vec_sum[1] = s.vec_sum[0] + s.vec_in[1]
-    send(vector_copy, 2)
-    reduce_step(1, 2)
-    vector_copy(2).wait_recv()
-    s.vec_planes[plane] = s.vec_sum[1] + s.vec_in[2]
-    for stage in (3, 4, 5):
-        send(vector_copy, stage)
-    reduce_step(3, 1)
-    reduce_step(2, 2)
-    reduce_finish(6, 0)
-    for stage in (3, 4, 5):
-        source = lax.rem(plane + 4 - (stage - 2), 4)
-        remote(
-            s.vec_planes.at[plane], s.vec_planes.at[source], (s.vec_sems.at[0, stage], s.vec_sems.at[1, stage]), beside
-        ).wait_recv()
-    total = s.vec_planes[0]
-    for each in range(1, 4):
-        total = total + s.vec_planes[each]
-    shares = pltpu.roll(total, lax.rem(WIDE - 32 * rank, WIDE), 1)[:, :BLOCK]
-    turned = pltpu.roll(total, lax.rem(WIDE - BLOCK * lax.rem(rank, 4), WIDE), 1)[:, :BLOCK]
+    for shift in range(1, CHIPS):
+        vector_copy(shift).start()
+    reduce_step(0, G_SELF)
+    reduce_step(0, G_LAST)
+    reduce_step(2, G_IN)
+    reduce_step(1, G_CROSS)
+    reduce_step(2, G_REST)
+    reduce_step(3, G_MORE)
+    lanes = pl.ds(pl.multiple_of(lax.div(chip, 2) * BLOCK, BLOCK), BLOCK)
+    total = s.vectors[:, lanes]
+    vector_all(0).wait_recv()
+    for shift in range(1, CHIPS):
+        total = total + s.vec_in[shift]
+    s.vec_four[0] = total
+    for other in range(3):
+        vector_copy(CHIPS + other).start()
+    reduce_step(2, G_EARLY)
+    reduce_step(1, G_LAST)
+    reduce_step(1, G_SELF)
+    reduce_step(3, G_IN)
+    reduce_step(2, G_CROSS)
+    reduce_step(3, G_REST)
+    vector_all(1).wait_recv()
+    total = (s.vec_four[0] + s.vec_four[2]) + (s.vec_four[1] + s.vec_four[3])
+    place_in_group = lax.rem(rank, 4)
+    s.final[pl.ds(AT_VECTORS, VECTOR_ROWS), :BLOCK] = pltpu.roll(total, lax.rem(BLOCK - 32 * place_in_group, BLOCK), 1)
     own = jnp.zeros((1, BLOCK), F32)
     for each in range(4):
-        own = own + jnp.where(lax.div(rank, 4) == each, turned[ROW_IN + each : ROW_IN + each + 1], 0.0)
-    s.final[pl.ds(AT_VECTORS, VECTOR_ROWS), :BLOCK] = shares
+        own = own + jnp.where(place_in_group == each, total[ROW_IN + each : ROW_IN + each + 1], 0.0)
     s.final[pl.ds(AT_VECTORS + ROW_IN, 1), :BLOCK] = own
     final_start(AT_VECTORS, VECTOR_ROWS)
 
@@ -1257,22 +1268,41 @@
     def put_final_unit(at, unit):
         final_put(at, unit_value(unit))
 
+    reduce_step(2, G_LAST)
+    reduce_step(2, G_SELF)
+    reduce_step(3, G_EARLY)
+    reduce_step(3, G_CROSS)
+    reduce_finish(6, G_OUT)
+    reduce_finish(6, G_MORE)
+    reduce_finish(6, G_IN)
+    reduce_finish(6, G_REST)
     for piece in range(4):
         put_final_unit(AT_OUT + 32 * piece, UNIT_OUT + piece)
         put_final_unit(AT_IN + 32 * piece, UNIT_IN + piece)
     final_start(AT_IN, 2 * BLOCK)
-    reduce_step(3, 2)
-    reduce_finish(6, 1)
+    reduce_finish(6, G_EARLY)
+    reduce_finish(6, G_CROSS)
     for which in (CO, CQ, CK, CV, SO):
         put_final_unit(AT_SQUARE + 32 * which, UNIT_OF[which])
-    reduce_finish(6, 2)
+    reduce_step(3, G_SELF)
+    reduce_step(3, G_LAST)
+    reduce_finish(6, G_SELF)
+    reduce_finish(6, G_LAST)
     for which in (SQ, SK, SV):
         put_final_unit(AT_SQUARE + 32 * which, UNIT_OF[which])
     final_start(AT_SQUARE, 256)
     for copy in finished:
         copy.wait()
-    for make in sent:
-        make().wait_send()
+    for group in range(len(SPANS)):
+        reduce_sent(6, group)
+    seven = pl.ds(0, CHIPS - 1)
+    for sent, blocks in (
+        (SENT_NARROW, s.narrow_out.at[:, seven]), (SENT_KV, s.kv_out.at[:, seven]), (SENT_DKV, s.dkv_out.at[:, seven]),
+        (SENT_PASS, s.kv.at[:, pl.ds(0, CHIPS)]), (SENT_SHARE, s.dkv_other),
+    ):
+        remote(blocks, blocks, (sent, s.vec_sems.at[0]), partner).wait_send()
+    vector_all(0).wait_send()
+    vector_all(1).wait_send()
 
 
 def place_kernel(packed, *refs):

time: 138 us -> 118 us (0.86)
  Pallas kernels: 137 us -> 117 us
    pallas_call x1, Pallas kernels: 134 us -> 114 us  [fused(): pl.pallas_call(fused_kernel, out_shape=jax.ShapeDtypeStruct((RESULT_ROWS,...]
where the time goes in v2:
time: 118 us
  Pallas kernels  117 us (99%)
    pallas_call x1, Pallas kernels, fused(): pl.pallas_call(fused_kernel, out_shape=jax.ShapeDtypeStruct((RESULT_ROWS,...  114 us
    pallas_call x1, Pallas kernels, fused(): pl.pallas_call(place_kernel, out_shape=shapes, in_specs=(PLACED,), out_sp...  2.87 us

profile of v2, /device:TPU:0, one launch (start us, length us, event | category | flops | bytes accessed | tf_op | source)
XLA Modules:
  0.0 118.0 jit_solution(860846125932540149)
XLA Ops:
  0.7 114.3 %shard_map.475.packed = f32[920,512]{1,0:T(8,128)} custom-call(bf16[128,512]{1,0:T(8,128)(2,1)} %bitcast.6, bf16[128,512]{1,0:T(8,128)(2,1)} %bitcast.7, s32[1,4]{1,0:T(1,128)} %refs_2_.1, bf16[128,512]{1,0:T(8,128)(2,1)} %bitcast.8, f32[512]{0:T(512)} %refs_4_.1, f32[512]{0:T(512)} %refs_5_.1, bf16[512,512]{1,0:T(8,128)(2,1)} %refs_6_.1, f32[512]{0:T(512)} %refs_7_.1, ...), custom_call_target="tpu_custom_call" | custom-call | tf_op jit(solution)/shard_map/pallas_call | solution.py:1341
  114.9 2.9 %shard_map.476 = (f32[128,512]{1,0:T(8,128)}, f32[128,512]{1,0:T(8,128)}, f32[128,512]{1,0:T(8,128)}, f32[32]{0:T(128)}, f32[32]{0:T(128)}, /*index=5*/f32[32,51...) custom-call(f32[920,512]{1,0:T(8,128)} %shard_map.475.packed), custom_call_target="tpu_custom_call" | custom-call | tf_op jit(solution)/shard_map/pallas_call | solution.py:1354

commit v3 on v2

--- a/solution.py
+++ b/solution.py
@@ -531,6 +531,7 @@
 MASKED = -1e30
 ONES_LANE = 5
 SELF, CROSS = 0, 1
+FAR_FIRST = (7, 6, 5, 4, 3, 2, 1)
 MESH = pl.DeviceIdType.MESH
 VMEM = pl.BlockSpec(memory_space=pltpu.VMEM)
 SMEM = pl.BlockSpec(memory_space=pltpu.SMEM)
@@ -546,9 +547,11 @@
 UNIT_OUT, UNIT_IN = 0, 4
 UNIT_OF = {CO: 8, SO: 9, CQ: 10, CK: 11, CV: 12, SQ: 13, SV: 14, SK: 15}
 UNITS = 16
-G_OUT, G_MORE, G_IN, G_REST, G_EARLY, G_CROSS, G_SELF, G_LAST = range(8)
-SPANS = ((0, 2), (2, 4), (4, 6), (6, 9), (9, 11), (11, 13), (13, 15), (15, 16))
-COLUMN_FIRST = (G_OUT, G_LAST)
+G_OUT, G_MORE, G_IN, G_REST, G_EARLY, G_CROSS, G_SQ, G_SV, G_SK = range(9)
+SPANS = ((0, 2), (2, 4), (4, 6), (6, 9), (9, 11), (11, 13), (13, 14), (14, 15), (15, 16))
+COLUMN_FIRST = (G_OUT, G_EARLY, G_SK)
+BY_CORE, BY_FIRST, BY_SECOND, BY_PLANES, BY_NEAR, BY_FAR, BY_HALVES = range(7)
+PLANES_IN_PAIRS = (G_OUT, G_MORE, G_IN, G_REST)
 X_SQ, X_SO, X_CQ, X_CO, X_CDO, X_CDQ, X_SDO, X_SDQ = range(8)
 
 
@@ -618,11 +621,12 @@
     grad_active: pltpu.VMEM((BLOCK, HIDDEN), F32)
     active: pltpu.VMEM((BLOCK, HIDDEN), BF16)
     grad_inner: pltpu.VMEM((BLOCK, HIDDEN), BF16)
-    parts: pltpu.VMEM((UNITS, 4, 2, 2, 2, ROUND, WIDE), BF16)
-    by_core: pltpu.VMEM((UNITS, 4, 2, 2, ROUND, WIDE), BF16)
-    by_side: pltpu.VMEM((UNITS, 4, 2, ROUND, WIDE), BF16)
-    by_column: pltpu.VMEM((UNITS, 4, ROUND, WIDE), BF16)
+    parts: pltpu.VMEM((UNITS, 2, 2, 2, 2, 2, ROUND, WIDE), BF16)
+    by_core: pltpu.VMEM((UNITS, 2, 2, 2, 2, ROUND, WIDE), BF16)
+    by_side: pltpu.VMEM((UNITS, 2, 2, 2, ROUND, WIDE), BF16)
+    by_column: pltpu.VMEM((UNITS, 2, 2, ROUND, WIDE), BF16)
     by_plane: pltpu.VMEM((3, UNITS, ROUND, WIDE), BF16)
+    by_near: pltpu.VMEM((UNITS, 2, ROUND, WIDE), BF16)
     halves: pltpu.VMEM((2, UNITS, ROUND, WIDE), BF16)
     vectors: pltpu.VMEM((VECTOR_ROWS, WIDE), F32)
     vec_in: pltpu.VMEM((CHIPS, VECTOR_ROWS, BLOCK), F32)
@@ -632,9 +636,9 @@
     kv_sems: pltpu.SemaphoreType.DMA((2, CHIPS))
     dkv_sems: pltpu.SemaphoreType.DMA((2,))
     pass_sems: pltpu.SemaphoreType.DMA((2,))
-    share_sems: pltpu.SemaphoreType.DMA((2, 2))
+    share_sems: pltpu.SemaphoreType.DMA((2, 4))
     sent_sems: pltpu.SemaphoreType.DMA((7,))
-    reduce_sems: pltpu.SemaphoreType.DMA((len(SPANS), 5))
+    reduce_sems: pltpu.SemaphoreType.DMA((len(SPANS), 7))
     reduce_sent: pltpu.SemaphoreType.DMA((len(SPANS),))
     vec_sems: pltpu.SemaphoreType.DMA((2,))
     final_sems: pltpu.SemaphoreType.DMA((6,))
@@ -686,8 +690,13 @@
     chip, core = lax.div(rank, 2), lax.rem(rank, 2)
     plane, column = lax.div(chip, 2), lax.rem(chip, 2)
 
-    def around(shift):
-        return lax.rem(chip + (CHIPS + shift), CHIPS)
+    plane_high, plane_low = lax.div(plane, 2), lax.rem(plane, 2)
+
+    def peer(turned):
+        high, low, side_by = (
+            1 - bit if turned >> at & 1 else bit for at, bit in ((2, plane_high), (1, plane_low), (0, column))
+        )
+        return 4 * high + 2 * low + side_by
 
     def at_rank(index):
         return {"blk": index}
@@ -733,7 +742,7 @@
 
     barrier = pltpu.get_barrier_semaphore()
     for shift in range(1, CHIPS):
-        pl.semaphore_signal(barrier, inc=1, device_id=at_rank(2 * around(shift) + core), device_id_type=MESH)
+        pl.semaphore_signal(barrier, inc=1, device_id=at_rank(2 * peer(shift) + core), device_id_type=MESH)
     for other in (partner, across, opposite):
         pl.semaphore_signal(barrier, inc=1, device_id=other, device_id_type=MESH)
 
@@ -749,13 +758,22 @@
             return (self.sent, self.sems.at[source] if self.by_source else self.sems)
 
         def start(self):
-            for shift in range(1, CHIPS):
-                to = around(shift)
+            for shift in FAR_FIRST:
+                to = peer(shift)
                 remote(self.outgoing.at[to], self.slot(chip), self.pair(chip), at_rank(2 * to + core)).start()
             self.slot(chip)[...] = self.outgoing[chip]
 
+        def start_to(self, to):
+            @pl.when(chip != to)
+            def _():
+                remote(self.outgoing.at[to], self.slot(chip), self.pair(chip), at_rank(2 * to + core)).start()
+
+            @pl.when(chip == to)
+            def _():
+                self.slot(chip)[...] = self.outgoing[to]
+
         def wait(self, shift):
-            source = around(-shift)
+            source = peer(shift)
             remote(
                 self.outgoing.at[source], self.slot(source), self.pair(source), at_rank(2 * source + core)
             ).wait_recv()
@@ -772,7 +790,7 @@
         for shift in range(CHIPS):
             if shift > 0:
                 keys_values[kind].wait(shift)
-            slot = s.kv.at[kind, 2 * around(-shift) + core]
+            slot = s.kv.at[kind, 2 * peer(shift) + core]
             remote(slot, slot, (SENT_PASS, s.pass_sems.at[kind]), partner).start()
 
     def pass_wait(kind):
@@ -809,74 +827,90 @@
         ]
         return tuple(jnp.concatenate(each, 1).astype(BF16) for each in zip(*pairs, strict=True))
 
-    def reduce_copy(stage, group):
+    def plane_rank(other):
+        return at_rank(2 * (2 * other + column) + core)
+
+    def reduce_copies(stage, group):
         first, last = SPANS[group]
         span = pl.ds(first, last - first)
-        sems = (s.reduce_sent.at[group], s.reduce_sems.at[group, {0: 0, 1: 1, 2: 2, 6: 4}.get(stage, 3)])
-        if stage == 0:
-            return remote(s.parts.at[span, :, :, 1 - core], s.by_core.at[span], sems, partner)
-        columns = (stage == 1) == (group in COLUMN_FIRST)
-        if stage == 1:
-            source = s.by_core.at[span, :, 1 - column] if columns else s.by_core.at[span, :, :, 1 - side]
-            return remote(source, s.by_side.at[span], sems, beside if columns else across)
-        if stage == 2:
-            source = s.by_side.at[span, :, 1 - column if columns else 1 - side]
-            return remote(source, s.by_column.at[span], sems, beside if columns else across)
-        if stage < 6:
-            to = lax.rem(plane + (stage - 2), 4)
-            return remote(
-                s.by_column.at[span, to], s.by_plane.at[stage - 3, span], sems, at_rank(2 * (2 * to + column) + core)
-            )
-        return remote(s.halves.at[side, span], s.halves.at[side, span], sems, across)
-
-    def planes_copy(group):
-        span = s.by_plane.at[:, pl.ds(SPANS[group][0], SPANS[group][1] - SPANS[group][0])]
-        return remote(span, span, (s.reduce_sent.at[group], s.reduce_sems.at[group, 3]), partner)
-
-    def reduce_sent(stage, group):
-        (planes_copy(group) if stage == 3 else reduce_copy(stage, group)).wait_send()
+        sems = (s.reduce_sent.at[group], s.reduce_sems.at[group, stage])
+        columns = (stage == BY_FIRST) == (group in COLUMN_FIRST)
+        if stage == BY_CORE:
+            return [remote(s.parts.at[span, :, :, :, 1 - core], s.by_core.at[span], sems, partner)]
+        if stage == BY_FIRST:
+            source = s.by_core.at[span, :, :, 1 - column] if columns else s.by_core.at[span, :, :, :, 1 - side]
+            return [remote(source, s.by_side.at[span], sems, beside if columns else across)]
+        if stage == BY_SECOND:
+            source = s.by_side.at[span, :, :, 1 - column if columns else 1 - side]
+            return [remote(source, s.by_column.at[span], sems, beside if columns else across)]
+        if stage == BY_PLANES:
+            others = [lax.rem(plane + shift, 4) for shift in range(1, 4)]
+            return [
+                remote(
+                    s.by_column.at[span, lax.div(to, 2), lax.rem(to, 2)], s.by_plane.at[at, span], sems, plane_rank(to)
+                )
+                for at, to in enumerate(others)
+            ]
+        if stage == BY_NEAR:
+            to = plane_rank(2 * plane_high + 1 - plane_low)
+            return [remote(s.by_column.at[span, :, 1 - plane_low], s.by_near.at[span], sems, to)]
+        if stage == BY_FAR:
+            to = plane_rank(2 * (1 - plane_high) + plane_low)
+            return [remote(s.by_near.at[span, 1 - plane_high], s.by_plane.at[0, span], sems, to)]
+        return [remote(s.halves.at[side, span], s.halves.at[side, span], sems, across)]
+
+    def reduce_whole(stage, group):
+        if stage != BY_PLANES:
+            return reduce_copies(stage, group)[0]
+        blocks = s.by_plane.at[:, pl.ds(SPANS[group][0], SPANS[group][1] - SPANS[group][0])]
+        return remote(blocks, blocks, (s.reduce_sent.at[group], s.reduce_sems.at[group, stage]), partner)
+
+    def reduce_next(stage, group):
+        if stage == BY_SECOND:
+            return BY_NEAR if group in PLANES_IN_PAIRS else BY_PLANES
+        return {BY_CORE: BY_FIRST, BY_FIRST: BY_SECOND, BY_NEAR: BY_FAR}.get(stage, BY_HALVES)
 
     def reduce_start(stage, group):
-        if stage > 0:
-            reduce_sent(3 if stage == 6 else stage - 1, group)
-        for each in (3, 4, 5) if stage == 3 else (stage,):
-            reduce_copy(each, group).start()
+        for copy in reduce_copies(stage, group):
+            copy.start()
 
     def reduce_finish(stage, group):
         first, last = SPANS[group]
-        if stage == 3:
-            planes_copy(group).wait_recv()
-        elif stage == 6:
+        if stage == BY_HALVES:
             half = s.halves.at[1 - side, pl.ds(first, last - first)]
-            remote(half, half, (s.reduce_sent.at[group], s.reduce_sems.at[group, 4]), across).wait_recv()
-        else:
-            reduce_copy(stage, group).wait_recv()
+            remote(half, half, (s.reduce_sent.at[group], s.reduce_sems.at[group, stage]), across).wait_recv()
+            return
+        reduce_whole(stage, group).wait_recv()
+        columns = (stage == BY_FIRST) == (group in COLUMN_FIRST)
 
         def add(unit, nothing):
-            if stage == 0:
-                s.by_core[unit] = s.by_core[unit] + s.parts[unit, :, :, core]
-            columns = (stage == 1) == (group in COLUMN_FIRST)
-            if stage == 1:
-                own = s.by_core[unit, :, column] if columns else s.by_core[unit, :, :, side]
+            if stage == BY_CORE:
+                s.by_core[unit] = s.by_core[unit] + s.parts[unit, :, :, :, core]
+            if stage == BY_FIRST:
+                own = s.by_core[unit, :, :, column] if columns else s.by_core[unit, :, :, :, side]
                 s.by_side[unit] = s.by_side[unit] + own
-            if stage == 2:
-                s.by_column[unit] = s.by_column[unit] + s.by_side[unit, :, column if columns else side]
-            if stage == 3:
-                total = s.by_column[unit, plane].astype(F32)
+            if stage == BY_SECOND:
+                s.by_column[unit] = s.by_column[unit] + s.by_side[unit, :, :, column if columns else side]
+            if stage == BY_PLANES:
+                total = s.by_column[unit, plane_high, plane_low].astype(F32)
                 for each in range(3):
                     total = total + s.by_plane[each, unit].astype(F32)
                 s.halves[side, unit] = total.astype(BF16)
+            if stage == BY_NEAR:
+                s.by_near[unit] = s.by_near[unit] + s.by_column[unit, :, plane_low]
+            if stage == BY_FAR:
+                s.halves[side, unit] = s.by_plane[0, unit] + s.by_near[unit, plane_high]
             return nothing
 
-        if stage < 6:
-            lax.fori_loop(first, last, add, 0)
+        lax.fori_loop(first, last, add, 0)
 
     def reduce_step(stage, group):
         reduce_finish(stage, group)
-        reduce_start(stage + 1 if stage < 3 else 6, group)
+        reduce_whole(stage, group).wait_send()
+        reduce_start(reduce_next(stage, group), group)
 
     def put_unit(unit, value):
-        s.parts[unit] = value.astype(BF16).reshape(4, 2, 2, 2, ROUND, WIDE)
+        s.parts[unit] = value.astype(BF16).reshape(2, 2, 2, 2, 2, ROUND, WIDE)
 
     def put_vector(row, values):
         if values.shape[1] == WIDE:
@@ -990,8 +1024,13 @@
                 s.dq_turned[:, rows] = toward if chunk == 0 else s.dq_turned[:, rows] + toward
             s.dkv_part[kind, 2 * chunk : 2 * chunk + 2] = total.astype(BF16).reshape(2, 2, BLOCK, BLOCK)
             between(chunk)
-        for block in range(CHIPS):
-            s.narrow_out[which_out, block] = (
+        if not causal:
+            for part in range(4):
+                put_dq(which_out, part)
+
+    def put_dq(which, part):
+        for block in (2 * part, 2 * part + 1):
+            s.narrow_out[which, block] = (
                 s.dq_turned[:HEAD, BLOCK * block : BLOCK * (block + 1)] * (HEAD**-0.5)
             ).astype(BF16)
 
@@ -999,17 +1038,16 @@
         return s.narrow[which].reshape(WIDE, BLOCK).astype(F32).T.astype(BF16)
 
     def share_copy(kind, part):
-        chips = pl.ds(4 * part, 4)
+        chips = pl.ds(2 * part, 2)
         return remote(
             s.dkv_part.at[kind, chips, 1 - core], s.dkv_other.at[kind, chips], (SENT_SHARE, s.share_sems.at[kind, part]),
             partner,
         )
 
-    def share_finish(kind):
-        for part in range(2):
-            share_copy(kind, part).wait_recv()
-            chips = slice(4 * part, 4 * part + 4)
-            s.dkv_out[kind, chips] = s.dkv_part[kind, chips, core] + s.dkv_other[kind, chips]
+    def share_finish(kind, part):
+        share_copy(kind, part).wait_recv()
+        chips = slice(2 * part, 2 * part + 2)
+        s.dkv_out[kind, chips] = s.dkv_part[kind, chips, core] + s.dkv_other[kind, chips]
 
     inputs = a.residues[...].astype(F32)
     normed = norm(inputs, 0, a.self_norm_gain, a.self_norm_bias)
@@ -1103,7 +1141,7 @@
     after_cross = after_self + dot_nn(cross_low, weight(CO)) + flat(a.cross_output_bias)
 
     normed = norm(after_cross, 2, a.feed_norm_gain, a.feed_norm_bias)
-    layer_out, back = after_cross + flat(a.feed_out_bias), None
+    back = None
     for piece in range(4):
         lanes = slice(512 * piece, 512 * (piece + 1))
         inner = dot_nn(normed, s.w_in[:, lanes]) + flat(a.feed_in_bias)[:, lanes]
@@ -1113,11 +1151,9 @@
         grad_inner = (s.grad_active[:, lanes] * slope).astype(BF16)
         s.active[:, lanes] = active
         s.grad_inner[:, lanes] = grad_inner
-        layer_out = layer_out + dot_nn(active, s.w_out[lanes, :])
         toward = dot_nt(grad_inner, s.w_in[:, lanes])
         back = toward if back is None else back + toward
-    final_put(AT_LAYER, layer_out)
-    final_start(AT_LAYER, BLOCK)
+    s.final[AT_LAYER : AT_LAYER + BLOCK, :] = after_cross + flat(a.feed_out_bias)
     upstream = a.cotangent[...].astype(F32)
     upstream = upstream + norm_gradient(back, 2, a.feed_norm_gain, ROW_FEED_GAIN)
 
@@ -1132,33 +1168,35 @@
         lanes = slice(512 * piece, 512 * (piece + 1))
         part = dot_tn(s.active[:, lanes], a.cotangent[...]).astype(BF16).reshape(2, 2, 4, 2, ROUND, WIDE)
         for each in range(4):
-            s.parts[UNIT_OUT + each, piece] = part[:, :, each]
-    reduce_start(0, G_OUT)
-    reduce_start(0, G_MORE)
+            s.parts[UNIT_OUT + each, piece // 2, piece % 2] = part[:, :, each]
+    reduce_start(BY_CORE, G_OUT)
+    reduce_start(BY_CORE, G_MORE)
     for piece in range(4):
         lanes = slice(512 * piece, 512 * (piece + 1))
         put_unit(UNIT_IN + piece, dot_tn(s.normed[2], s.grad_inner[:, lanes]))
         if piece == 1:
-            reduce_start(0, G_IN)
+            reduce_start(BY_CORE, G_IN)
+            reduce_step(BY_CORE, G_MORE)
     put_unit(UNIT_OF[CO], dot_tn(s.attended[CROSS], branch))
-    reduce_start(0, G_REST)
-    reduce_step(0, G_MORE)
+    reduce_start(BY_CORE, G_REST)
+    final_put(AT_LAYER, s.final[AT_LAYER : AT_LAYER + BLOCK, :] + dot_nn(s.active[...], s.w_out[...]))
+    final_start(AT_LAYER, BLOCK)
     narrow[X_CDO].wait_all()
-    reduce_step(0, G_OUT)
+    reduce_step(BY_CORE, G_OUT)
 
     def between_cross(chunk):
         if chunk == 0:
-            reduce_step(0, G_IN)
-        if chunk in (1, 3):
-            share_copy(CROSS, chunk // 2).start()
+            reduce_step(BY_CORE, G_IN)
+        share_copy(CROSS, chunk).start()
 
     attend_back(CROSS, False, X_CDO, X_CDQ, between_cross)
     narrow[X_CDQ].start()
-    share_finish(CROSS)
+    for part in range(4):
+        share_finish(CROSS, part)
     key_grads[CROSS].start()
-    reduce_step(1, G_OUT)
-    reduce_step(0, G_REST)
-    reduce_step(1, G_MORE)
+    reduce_step(BY_FIRST, G_OUT)
+    reduce_step(BY_CORE, G_REST)
+    reduce_step(BY_FIRST, G_MORE)
     narrow[X_CDQ].wait_all()
     grad_query = turned_rows(X_CDQ)
     gradient = dot_nt(grad_query, weight(CQ))
@@ -1167,58 +1205,76 @@
     branch = upstream.astype(BF16)
     pack_groups(dot_nt(branch, weight(SO)), X_SDO)
     narrow[X_SDO].start()
-    reduce_step(2, G_OUT)
-    reduce_step(1, G_IN)
+    reduce_step(BY_SECOND, G_OUT)
+    reduce_step(BY_FIRST, G_IN)
     s.upstream[...] = upstream
     put_vector(ROW_SO, column_sum(branch))
     put_vector(ROW_CQ, column_sum(grad_query))
     put_unit(UNIT_OF[SO], dot_tn(s.attended[SELF], branch))
     put_unit(UNIT_OF[CQ], dot_tn(s.normed[1], grad_query))
-    reduce_start(0, G_EARLY)
+    reduce_start(BY_CORE, G_EARLY)
     key_grads[CROSS].wait_all()
     grad_key, grad_value = unpack_pairs(CROSS)
     put_vector(ROW_CV, column_sum(grad_value))
     put_unit(UNIT_OF[CK], dot_tn(a.memory[...], grad_key))
     put_unit(UNIT_OF[CV], dot_tn(a.memory[...], grad_value))
-    reduce_start(0, G_CROSS)
-    reduce_step(0, G_EARLY)
+    reduce_start(BY_CORE, G_CROSS)
+    reduce_step(BY_CORE, G_EARLY)
     final_put(AT_MEMORY, dot_nt(grad_key, weight(CK)) + dot_nt(grad_value, weight(CV)))
     final_start(AT_MEMORY, BLOCK)
     narrow[X_SDO].wait_all()
-    reduce_step(2, G_MORE)
-    reduce_step(1, G_REST)
+    reduce_step(BY_SECOND, G_MORE)
+    reduce_step(BY_FIRST, G_REST)
 
     def between_self(chunk):
+        put_dq(X_SDQ, chunk)
+        share_copy(SELF, chunk).start()
+        if chunk > 0:
+            send_shares(chunk - 1)
+        for to in (2 * chunk, 2 * chunk + 1):
+            narrow[X_SDQ].start_to(to)
         if chunk == 0:
-            reduce_step(0, G_CROSS)
-        if chunk in (1, 3):
-            share_copy(SELF, chunk // 2).start()
+            reduce_step(BY_CORE, G_CROSS)
+            reduce_step(BY_NEAR, G_OUT)
+        if chunk == 1:
+            reduce_step(BY_SECOND, G_IN)
+
+    def send_shares(part):
+        share_finish(SELF, part)
+        for to in (2 * part, 2 * part + 1):
+            key_grads[SELF].start_to(to)
 
     attend_back(SELF, True, X_SDO, X_SDQ, between_self)
-    narrow[X_SDQ].start()
-    share_finish(SELF)
-    key_grads[SELF].start()
-    reduce_step(3, G_OUT)
+    send_shares(3)
+    reduce_step(BY_NEAR, G_MORE)
+    reduce_step(BY_FAR, G_OUT)
+    reduce_step(BY_FIRST, G_EARLY)
+    reduce_step(BY_FIRST, G_CROSS)
     narrow[X_SDQ].wait_all()
     grad_query = turned_rows(X_SDQ)
-    put_unit(UNIT_OF[SQ], dot_tn(s.normed[0], grad_query))
-    reduce_step(1, G_EARLY)
+    normed = s.normed[0]
+    put_unit(UNIT_OF[SQ], dot_tn(normed, grad_query))
+    reduce_start(BY_CORE, G_SQ)
+    reduce_step(BY_SECOND, G_REST)
+    reduce_step(BY_NEAR, G_IN)
+    reduce_step(BY_CORE, G_SQ)
     key_grads[SELF].wait_all()
     grad_key, grad_value = unpack_pairs(SELF)
-    normed = s.normed[0]
     put_unit(UNIT_OF[SV], dot_tn(normed, grad_value))
-    reduce_start(0, G_SELF)
+    reduce_start(BY_CORE, G_SV)
     put_unit(UNIT_OF[SK], dot_tn(normed, grad_key))
-    reduce_start(0, G_LAST)
+    reduce_start(BY_CORE, G_SK)
     put_vector(ROW_SQ, column_sum(grad_query))
     put_vector(ROW_SV, column_sum(grad_value))
     gradient = dot_nt(grad_query, weight(SQ)) + dot_nt(grad_key, weight(SK)) + dot_nt(grad_value, weight(SV))
+    reduce_step(BY_CORE, G_SV)
+    reduce_step(BY_CORE, G_SK)
     final_put(AT_RESIDUES, s.upstream[...] + norm_gradient(gradient, 0, a.self_norm_gain, ROW_SELF_GAIN))
     final_start(AT_RESIDUES, BLOCK)
 
     def vector_copy(shift):
         if shift < CHIPS:
-            to = around(shift)
+            to = peer(shift)
             lanes = pl.ds(pl.multiple_of(lax.div(to, 2) * BLOCK, BLOCK), BLOCK)
             sems = (SENT_VECTOR, s.vec_sems.at[0])
             return remote(s.vectors.at[:, lanes], s.vec_in.at[shift], sems, at_rank(2 * to + core))
@@ -1230,14 +1286,14 @@
         return remote(rows, rows, ((SENT_VECTOR, SENT_FOUR)[step], s.vec_sems.at[step]), partner)
 
     s.vectors[pl.ds(17, VECTOR_ROWS - 17), :] = jnp.zeros((VECTOR_ROWS - 17, WIDE), F32)
-    for shift in range(1, CHIPS):
+    for shift in FAR_FIRST:
         vector_copy(shift).start()
-    reduce_step(0, G_SELF)
-    reduce_step(0, G_LAST)
-    reduce_step(2, G_IN)
-    reduce_step(1, G_CROSS)
-    reduce_step(2, G_REST)
-    reduce_step(3, G_MORE)
+    reduce_step(BY_SECOND, G_EARLY)
+    reduce_step(BY_SECOND, G_CROSS)
+    reduce_step(BY_NEAR, G_REST)
+    reduce_step(BY_FAR, G_MORE)
+    reduce_step(BY_FAR, G_IN)
+    reduce_step(BY_FIRST, G_SQ)
     lanes = pl.ds(pl.multiple_of(lax.div(chip, 2) * BLOCK, BLOCK), BLOCK)
     total = s.vectors[:, lanes]
     vector_all(0).wait_recv()
@@ -1246,12 +1302,10 @@
     s.vec_four[0] = total
     for other in range(3):
         vector_copy(CHIPS + other).start()
-    reduce_step(2, G_EARLY)
-    reduce_step(1, G_LAST)
-    reduce_step(1, G_SELF)
-    reduce_step(3, G_IN)
-    reduce_step(2, G_CROSS)
-    reduce_step(3, G_REST)
+    reduce_step(BY_FIRST, G_SK)
+    reduce_step(BY_FIRST, G_SV)
+    reduce_step(BY_PLANES, G_EARLY)
+    reduce_step(BY_SECOND, G_SQ)
     vector_all(1).wait_recv()
     total = (s.vec_four[0] + s.vec_four[2]) + (s.vec_four[1] + s.vec_four[3])
     place_in_group = lax.rem(rank, 4)
@@ -1268,33 +1322,33 @@
     def put_final_unit(at, unit):
         final_put(at, unit_value(unit))
 
-    reduce_step(2, G_LAST)
-    reduce_step(2, G_SELF)
-    reduce_step(3, G_EARLY)
-    reduce_step(3, G_CROSS)
-    reduce_finish(6, G_OUT)
-    reduce_finish(6, G_MORE)
-    reduce_finish(6, G_IN)
-    reduce_finish(6, G_REST)
+    reduce_step(BY_SECOND, G_SK)
+    reduce_step(BY_SECOND, G_SV)
+    reduce_step(BY_FAR, G_REST)
+    reduce_step(BY_PLANES, G_CROSS)
+    reduce_step(BY_PLANES, G_SQ)
+    for group in (G_OUT, G_MORE, G_IN, G_REST):
+        reduce_finish(BY_HALVES, group)
     for piece in range(4):
         put_final_unit(AT_OUT + 32 * piece, UNIT_OUT + piece)
         put_final_unit(AT_IN + 32 * piece, UNIT_IN + piece)
     final_start(AT_IN, 2 * BLOCK)
-    reduce_finish(6, G_EARLY)
-    reduce_finish(6, G_CROSS)
+    reduce_finish(BY_HALVES, G_EARLY)
+    reduce_finish(BY_HALVES, G_CROSS)
     for which in (CO, CQ, CK, CV, SO):
         put_final_unit(AT_SQUARE + 32 * which, UNIT_OF[which])
-    reduce_step(3, G_SELF)
-    reduce_step(3, G_LAST)
-    reduce_finish(6, G_SELF)
-    reduce_finish(6, G_LAST)
+    reduce_step(BY_PLANES, G_SK)
+    reduce_step(BY_PLANES, G_SV)
+    reduce_finish(BY_HALVES, G_SQ)
+    reduce_finish(BY_HALVES, G_SK)
+    reduce_finish(BY_HALVES, G_SV)
     for which in (SQ, SK, SV):
         put_final_unit(AT_SQUARE + 32 * which, UNIT_OF[which])
     final_start(AT_SQUARE, 256)
     for copy in finished:
         copy.wait()
     for group in range(len(SPANS)):
-        reduce_sent(6, group)
+        reduce_whole(BY_HALVES, group).wait_send()
     seven = pl.ds(0, CHIPS - 1)
     for sent, blocks in (
         (SENT_NARROW, s.narrow_out.at[:, seven]), (SENT_KV, s.kv_out.at[:, seven]), (SENT_DKV, s.dkv_out.at[:, seven]),

time: 118 us -> 112 us (0.949)
  Pallas kernels: 117 us -> 111 us
    pallas_call x1, Pallas kernels: 114 us -> 108 us  [fused(): pl.pallas_call(fused_kernel, out_shape=jax.ShapeDtypeStruct((RESULT_ROWS,...]
where the time goes in v3:
time: 112 us
  Pallas kernels  111 us (99%)
    pallas_call x1, Pallas kernels, fused(): pl.pallas_call(fused_kernel, out_shape=jax.ShapeDtypeStruct((RESULT_ROWS,...  108 us
    pallas_call x1, Pallas kernels, fused(): pl.pallas_call(place_kernel, out_shape=shapes, in_specs=(PLACED,), out_sp...  2.87 us

profile of v3, /device:TPU:0, one launch (start us, length us, event | category | flops | bytes accessed | tf_op | source)
XLA Modules:
  0.0 112.0 jit_solution(13504797522813113454)
XLA Ops:
  0.7 108.3 %shard_map.475.packed = f32[920,512]{1,0:T(8,128)} custom-call(bf16[128,512]{1,0:T(8,128)(2,1)} %bitcast.6, bf16[128,512]{1,0:T(8,128)(2,1)} %bitcast.7, s32[1,4]{1,0:T(1,128)} %refs_2_.1, bf16[128,512]{1,0:T(8,128)(2,1)} %bitcast.8, f32[512]{0:T(512)} %refs_4_.1, f32[512]{0:T(512)} %refs_5_.1, bf16[512,512]{1,0:T(8,128)(2,1)} %refs_6_.1, f32[512]{0:T(512)} %refs_7_.1, ...), custom_call_target="tpu_custom_call" | custom-call | tf_op jit(solution)/shard_map/pallas_call | solution.py:1395
  109.0 2.9 %shard_map.476 = (f32[128,512]{1,0:T(8,128)}, f32[128,512]{1,0:T(8,128)}, f32[128,512]{1,0:T(8,128)}, f32[32]{0:T(128)}, f32[32]{0:T(128)}, /*index=5*/f32[32,51...) custom-call(f32[920,512]{1,0:T(8,128)} %shard_map.475.packed), custom_call_target="tpu_custom_call" | custom-call | tf_op jit(solution)/shard_map/pallas_call | solution.py:1408

commit v4 on v3

--- a/solution.py
+++ b/solution.py
@@ -531,7 +531,7 @@
 MASKED = -1e30
 ONES_LANE = 5
 SELF, CROSS = 0, 1
-FAR_FIRST = (7, 6, 5, 4, 3, 2, 1)
+FAR_FIRST = (5, 7, 4, 6, 1, 3, 2)
 MESH = pl.DeviceIdType.MESH
 VMEM = pl.BlockSpec(memory_space=pltpu.VMEM)
 SMEM = pl.BlockSpec(memory_space=pltpu.SMEM)
@@ -1182,10 +1182,10 @@
     final_put(AT_LAYER, s.final[AT_LAYER : AT_LAYER + BLOCK, :] + dot_nn(s.active[...], s.w_out[...]))
     final_start(AT_LAYER, BLOCK)
     narrow[X_CDO].wait_all()
-    reduce_step(BY_CORE, G_OUT)
 
     def between_cross(chunk):
         if chunk == 0:
+            reduce_step(BY_CORE, G_OUT)
             reduce_step(BY_CORE, G_IN)
         share_copy(CROSS, chunk).start()
 

time: 112 us -> 112 us (level)
  no operation moved by 1% of the time
where the time goes in v4:
time: 112 us; the launch traced here: 111 us
  Pallas kernels  111 us (99%)
    pallas_call x1, Pallas kernels, fused(): pl.pallas_call(fused_kernel, out_shape=jax.ShapeDtypeStruct((RESULT_ROWS,...  108 us
    pallas_call x1, Pallas kernels, fused(): pl.pallas_call(place_kernel, out_shape=shapes, in_specs=(PLACED,), out_sp...  2.87 us

profile of v4, /device:TPU:0, one launch (start us, length us, event | category | flops | bytes accessed | tf_op | source)
XLA Modules:
  0.0 111.5 jit_solution(7741327901542184883)
XLA Ops:
  0.7 107.7 %shard_map.475.packed = f32[920,512]{1,0:T(8,128)} custom-call(bf16[128,512]{1,0:T(8,128)(2,1)} %bitcast.6, bf16[128,512]{1,0:T(8,128)(2,1)} %bitcast.7, s32[1,4]{1,0:T(1,128)} %refs_2_.1, bf16[128,512]{1,0:T(8,128)(2,1)} %bitcast.8, f32[512]{0:T(512)} %refs_4_.1, f32[512]{0:T(512)} %refs_5_.1, bf16[512,512]{1,0:T(8,128)(2,1)} %refs_6_.1, f32[512]{0:T(512)} %refs_7_.1, ...), custom_call_target="tpu_custom_call" | custom-call | tf_op jit(solution)/shard_map/pallas_call | solution.py:1395
  108.4 2.9 %shard_map.476 = (f32[128,512]{1,0:T(8,128)}, f32[128,512]{1,0:T(8,128)}, f32[128,512]{1,0:T(8,128)}, f32[32]{0:T(128)}, f32[32]{0:T(128)}, /*index=5*/f32[32,51...) custom-call(f32[920,512]{1,0:T(8,128)} %shard_map.475.packed), custom_call_target="tpu_custom_call" | custom-call | tf_op jit(solution)/shard_map/pallas_call | solution.py:1408
